TPU v7x, 512 devices: a whole 4x8x8 slice. The times are simulated.
512 devices in a mesh: pipe: 16 (over y, x_lo), expert: 16 (over z, core), dp: 2 (over x_hi).
Axes of the slice: x: 4 (x_hi: 2, x_lo: 2; x = x_hi * 2 + x_lo), y: 8, z: 8, core: 2. Of those that a mesh axis runs over, the one named last changes fastest.
Arguments:
- forward_input: bfloat16 [16, 2048, 3584], P('pipe', 'expert', 'dp'), may hold values from -6 to 6
- saved_input: bfloat16 [16, 2048, 3584], P('pipe', 'expert', 'dp'), may hold values from -6 to 6
- output_grad: bfloat16 [16, 2048, 3584], P('pipe', 'expert', 'dp'), may hold values from -6 to 6
- gate_proj: bfloat16 [16, 3584, 4096], P('pipe', 'dp', 'expert'), may hold values from -0.09375 to 0.09375
- up_proj: bfloat16 [16, 3584, 4096], P('pipe', 'dp', 'expert'), may hold values from -0.09375 to 0.09375
- down_proj: bfloat16 [16, 4096, 3584], P('pipe', 'expert', 'dp'), may hold values from -0.125 to 0.125
- affinity: float32 [2, 16, 2048, 8], P(None, 'pipe', 'expert'), may hold values from 0.05 to 1
- token_lists: int32 [2, 16, 16, 2, 16], P(None, 'pipe', 'expert'), may hold values from -1 to 127, as said below
- slot_ids: int32 [2, 16, 16, 2, 16], P(None, 'pipe', 'expert'), may hold values from 0 to 7, as said below
Outputs:
- next_section_input: bfloat16 [16, 2048, 3584], P('pipe', 'expert', 'dp')
- prev_section_grad: bfloat16 [16, 2048, 3584], P('pipe', 'expert', 'dp')
Inputs may be any that keep to these rules, and one draw needn't show every extreme that they name: `token_lists`: an entry is an index into the 128 tokens of source index j, or -1. The live entries of one list are distinct and come first, then -1 to the end. In every block and section one expert's lists are full from every source; the others hold 1 to 16 tokens. `slot_ids`: where a token stands in the lists of several experts of one block and section, their slots differ. The entry is 0 where the list entry is -1.
All inputs are finite; a program needn't handle non-finite values.
Results may differ from a plain program's by a relative error of at most 0.0064.
Values may be sent and summed in bfloat16 or wider, within the bound.
A program may use at most 64 MiB of HBM per device.

v0:
```python
import jax
import jax.numpy as jnp
from jax import lax
from jax.sharding import PartitionSpec as P

EXPERTS = 2


ROUTED_SCALE = 2.5


def shifted(shard, axis, by):
    peers = lax.axis_size(axis)
    return lax.ppermute(shard, axis, [(i, (i + by) % peers) for i in range(peers)])


def pick_rows(source, token_list):
    live_mask = token_list >= 0
    row_index = jnp.where(live_mask, token_list, 0)
    picked = jnp.take(source, row_index, axis=0)
    return jnp.where(live_mask[..., None], picked, jnp.zeros_like(picked))


def entry_weights(section_affinity, token_list, slot_list):
    live_mask = token_list >= 0
    row_index = jnp.where(live_mask, token_list, 0)
    normalized = section_affinity / jnp.sum(section_affinity, axis=1, keepdims=True)
    return jnp.where(live_mask, ROUTED_SCALE * normalized[row_index, slot_list], 0.0)


def place_rows(values, token_list, token_count):
    live_mask = token_list >= 0
    row_index = jnp.where(live_mask, token_list, token_count).reshape(-1)
    flat_rows = values.reshape(-1, values.shape[-1])
    total = jnp.zeros((token_count, values.shape[-1]), jnp.float32)
    return total.at[row_index].add(flat_rows, mode="drop")


def per_device(
    forward_input,
    saved_input,
    output_grad,
    gate_proj,
    up_proj,
    down_proj,
    affinity,
    token_lists,
    slot_ids,
):
    section_forward = forward_input[0]
    section_saved = saved_input[0]
    section_grad = output_grad[0]
    w_gate = gate_proj[0]
    w_up = up_proj[0]
    w_down = down_proj[0]
    token_count = section_forward.shape[0]
    copies = lax.axis_size("expert") // EXPERTS
    list_fwd = token_lists[0, 0, 0]
    list_bwd = token_lists[1, 0, 0]
    weight_fwd = entry_weights(affinity[0, 0], list_fwd, slot_ids[0, 0, 0])
    weight_bwd = entry_weights(affinity[1, 0], list_bwd, slot_ids[1, 0, 0])
    sent_fwd = jnp.repeat(pick_rows(section_forward, list_fwd), copies, axis=0)
    sent_bwd = jnp.repeat(pick_rows(section_saved, list_bwd), copies, axis=0)
    weighted = (
        weight_bwd[..., None] * pick_rows(section_grad, list_bwd).astype(jnp.float32)
    ).astype(jnp.bfloat16)
    sent_grad = jnp.repeat(weighted, copies, axis=0)

    def gate_in(picked):
        return jnp.einsum("jkd,df->jkf", picked, w_gate, preferred_element_type=jnp.float32)

    def up_in(picked):
        return jnp.einsum("jkd,df->jkf", picked, w_up, preferred_element_type=jnp.float32)

    def collect(partials):
        shaped = partials.reshape(EXPERTS, copies, partials.shape[1], partials.shape[2])
        return jnp.sum(shaped.astype(jnp.float32), axis=1)

    rows_fwd = lax.all_to_all(sent_fwd, "expert", split_axis=0, concat_axis=0, tiled=True)
    gate_fwd, up_fwd = lax.psum((gate_in(rows_fwd), up_in(rows_fwd)), "dp")
    hidden = (jax.nn.silu(gate_fwd) * up_fwd).astype(jnp.bfloat16)
    back_fwd = lax.all_to_all(
        jnp.einsum("jkf,fd->jkd", hidden, w_down, preferred_element_type=jnp.float32).astype(
            jnp.bfloat16
        ),
        "expert",
        split_axis=0,
        concat_axis=0,
        tiled=True,
    )
    rows_bwd, grad_rows = (
        lax.all_to_all(sent_bwd, "expert", split_axis=0, concat_axis=0, tiled=True),
        lax.all_to_all(sent_grad, "expert", split_axis=0, concat_axis=0, tiled=True),
    )
    gate_bwd, up_bwd, grad_hidden = lax.psum(
        (
            gate_in(rows_bwd),
            up_in(rows_bwd),
            jnp.einsum("jkd,fd->jkf", grad_rows, w_down, preferred_element_type=jnp.float32),
        ),
        "dp",
    )
    sigma_gate = jax.nn.sigmoid(gate_bwd)
    grad_gate = (grad_hidden * up_bwd * sigma_gate * (1.0 + gate_bwd * (1.0 - sigma_gate))).astype(
        jnp.bfloat16
    )
    grad_up = (grad_hidden * gate_bwd * sigma_gate).astype(jnp.bfloat16)
    first_term = jnp.einsum("jkf,df->jkd", grad_gate, w_gate, preferred_element_type=jnp.float32)
    back_bwd = lax.all_to_all(
        (
            first_term
            + jnp.einsum("jkf,df->jkd", grad_up, w_up, preferred_element_type=jnp.float32)
        ).astype(jnp.bfloat16),
        "expert",
        split_axis=0,
        concat_axis=0,
        tiled=True,
    )
    layer_out = place_rows(weight_fwd[..., None] * collect(back_fwd), list_fwd, token_count).astype(
        jnp.bfloat16
    )
    input_grad = place_rows(collect(back_bwd), list_bwd, token_count).astype(jnp.bfloat16)
    next_section_input = shifted(layer_out[None], "pipe", 1)
    prev_section_grad = shifted(input_grad[None], "pipe", -1)
    return (next_section_input, prev_section_grad)


def solution(mesh):
    in_specs = (
        P("pipe", "expert", "dp"),
        P("pipe", "expert", "dp"),
        P("pipe", "expert", "dp"),
        P("pipe", "dp", "expert"),
        P("pipe", "dp", "expert"),
        P("pipe", "expert", "dp"),
        P(None, "pipe", "expert", None),
        P(None, "pipe", "expert", None, None),
        P(None, "pipe", "expert", None, None),
    )
    out_specs = (P("pipe", "expert", "dp"), P("pipe", "expert", "dp"))
    return jax.shard_map(
        per_device, mesh=mesh, in_specs=in_specs, out_specs=out_specs, check_vma=False
    )
```

profile of v0, /device:TPU:1, one launch (start us, length us, event | category | flops | bytes accessed | tf_op | source)
XLA Modules:
  0.0 263.6 jit_solution(8049072777379460036)
XLA Ops:
  7.2 0.0 copy-start
  7.2 0.0 copy-start.4
  7.2 0.8 slice_reduce_fusion
  8.0 0.7 fusion.24
  8.8 0.1 reshape.266
  8.8 0.7 bitcast_divide_fusion.1
  9.5 0.7 gather_fusion.1
  10.2 0.1 reshape.297
  10.3 0.7 broadcast_select_fusion
  11.0 0.7 compare_and_fusion
  11.7 0.1 reshape.303
  11.8 0.1 reshape.299
  11.9 1.8 gather_fusion.2
  13.7 0.0 copy-done.4
  13.7 0.6 gather_fusion.4
  14.4 0.1 select_select_fusion
  14.5 0.1 broadcast_in_dim.81
  14.6 37.4 %all_to_all.25 = bf16[16,16,1792]{2,1,0:T(8,128)(2,1)S(1)} all-to-all(bf16[16,16,1792]{2,1,0:T(8,128)(2,1)S(1)} %bitcast.86), channel_id=1, replica_groups=mesh['pipe'=16,'expert'=16,'dp'=2] {'expert'}, dimensions={0} | all-to-all | bytes 1835008 | tf_op jit(solution)/shard_map/all_to_all | solution.py:92
  51.9 1.0 broadcast_in_dim.76
  52.9 3.5 %all-to-all-start = ((bf16[16,16,1792]{2,1,0:T(8,128)(2,1)}), bf16[16,16,1792]{2,1,0:T(8,128)(2,1)S(1)}, u32[]{:S(2)}, u32[]{:S(2)}) async-start(bf16[16,16,1792]{2,1,0:T(8,128)(2,1)} %bitcast.84), calls=%async_computation | async-start | bytes 1835008 | tf_op jit(solution)/shard_map/all_to_all | solution.py:79
  56.5 0.0 copy-done.5
  56.5 0.6 gather_fusion.3
  57.1 0.1 multiply_convert_fusion.3
  57.2 23.9 %all-to-all-done = bf16[16,16,1792]{2,1,0:T(8,128)(2,1)S(1)} async-done(((bf16[16,16,1792]{2,1,0:T(8,128)(2,1)}), bf16[16,16,1792]{2,1,0:T(8,128)(2,1)S(1)}, u32[]{:S(2)}, u32[]{:S(2)}) %all-to-all-start) | async-done | bytes 917536 | tf_op jit(solution)/shard_map/all_to_all | solution.py:79
  81.1 1.0 broadcast_in_dim.80
  82.1 4.2 %all-to-all-start.2 = ((bf16[16,16,1792]{2,1,0:T(8,128)(2,1)}), bf16[16,16,1792]{2,1,0:T(8,128)(2,1)}, u32[]{:S(2)}, u32[]{:S(2)}) async-start(bf16[16,16,1792]{2,1,0:T(8,128)(2,1)} %bitcast.85), calls=%async_computation.2 | async-start | bytes 1835008 | tf_op jit(solution)/shard_map/all_to_all | solution.py:93
  86.3 0.0 all-reduce.3.cloned.1.call-start
  86.3 0.0 copy-done
  86.4 0.0 copy-start.1
  86.4 1.1 fusion.11
  87.5 0.1 copy-done.1
  87.5 1.1 fusion.5
  88.7 1.1 fusion.7
  89.8 1.1 fusion.13
  90.9 20.0 %all-to-all-done.2 = bf16[16,16,1792]{2,1,0:T(8,128)(2,1)} async-done(((bf16[16,16,1792]{2,1,0:T(8,128)(2,1)}), bf16[16,16,1792]{2,1,0:T(8,128)(2,1)}, u32[]{:S(2)}, u32[]{:S(2)}) %all-to-all-start.2) | async-done | bytes 917536 | tf_op jit(solution)/shard_map/all_to_all | solution.py:93
  110.8 0.0 copy-done.3
  110.8 2.3 fusion.1
  113.2 0.0 all-reduce.3.cloned.1.call-update
  113.2 62.5 %all-reduce.3.cloned.1.call-done = (f32[16,16,256]{2,1,0:T(8,128)}, f32[16,16,256]{2,1,0:T(8,128)}, f32[16,16,256]{2,1,0:T(8,128)}, f32[16,16,256]{2,1,0:T(8,128)}, f32[16,16,256]{2,1,0:T(8,128)}) async-done(((f32[16,16,256]{2,1,0:T(8,128)}, f32[16,16,256]{2,1,0:T(8,128)}, f32[16,16,256]{2,1,0:T(8,128)}, f32[16,16,256]{2,1,0:T(8,128)}, f32[16,16,256]{2,1,0:T(8,128)}), (f32[16,16,256]{2,1,0:T(8,128)}, ...) | async-done | bytes 1310736 | tf_op jit(solution)/shard_map/psum | solution.py:80
  175.7 2.4 convolution_convert_fusion
  178.1 8.2 %all-to-all-start.1 = ((bf16[16,16,1792]{2,1,0:T(8,128)(2,1)}), bf16[16,16,1792]{2,1,0:T(8,128)(2,1)S(1)}, u32[]{:S(2)}, u32[]{:S(2)}) async-start(bf16[16,16,1792]{2,1,0:T(8,128)(2,1)} %convolution_convert_fusion), calls=%async_computation.1 | async-start | bytes 1835008 | tf_op jit(solution)/shard_map/all_to_all | solution.py:82
  186.4 0.1 ge.73
  186.4 0.1 reshape.260
  186.5 0.1 squeeze.53
  186.6 0.1 squeeze.44
  186.7 0.7 gather_fusion
  187.4 0.5 fusion.9
  187.9 0.7 copy-done.2
  188.5 1.4 fusion
  189.9 21.7 %all-to-all-done.1 = bf16[16,16,1792]{2,1,0:T(8,128)(2,1)S(1)} async-done(((bf16[16,16,1792]{2,1,0:T(8,128)(2,1)}), bf16[16,16,1792]{2,1,0:T(8,128)(2,1)S(1)}, u32[]{:S(2)}, u32[]{:S(2)}) %all-to-all-start.1) | async-done | bytes 917536 | tf_op jit(solution)/shard_map/all_to_all | solution.py:82
  211.6 3.5 %all-to-all-start.4 = ((bf16[16,16,1792]{2,1,0:T(8,128)(2,1)}), bf16[16,16,1792]{2,1,0:T(8,128)(2,1)S(1)}, u32[]{:S(2)}, u32[]{:S(2)}) async-start(bf16[16,16,1792]{2,1,0:T(8,128)(2,1)} %fusion), calls=%async_computation.4 | async-start | bytes 1835008 | tf_op jit(solution)/shard_map/all_to_all | solution.py:109
  215.2 0.1 convert_reduce_fusion.1
  215.3 0.1 bitcast_multiply_fusion
  215.4 1.2 scatter_custom_fusion
  216.6 0.8 convert_bitcast_fusion.1
  217.4 2.2 collective-permute-start
  219.6 20.7 %all-to-all-done.4 = bf16[16,16,1792]{2,1,0:T(8,128)(2,1)S(1)} async-done(((bf16[16,16,1792]{2,1,0:T(8,128)(2,1)}), bf16[16,16,1792]{2,1,0:T(8,128)(2,1)S(1)}, u32[]{:S(2)}, u32[]{:S(2)}) %all-to-all-start.4) | async-done | bytes 917536 | tf_op jit(solution)/shard_map/all_to_all | solution.py:109
  240.3 0.1 convert_reduce_fusion
  240.4 1.2 scatter_custom_fusion.1
  241.6 4.5 %collective-permute-start.1 = (bf16[1,128,1792]{2,1,0:T(8,128)(2,1)S(1)}, bf16[1,128,1792]{2,1,0:T(8,128)(2,1)S(1)}, u32[]{:S(2)}, u32[]{:S(2)}) collective-permute-start(bf16[1,128,1792]{2,1,0:T(8,128)(2,1)S(1)} %convert_bitcast_fusion), channel_id=1, source_target_pairs={{0,480},{32,0},{64,32},{96,64},{128,96},{160,128},{192,160},{224,1... | collective-permute-start | bytes 1376264 | tf_op jit(solution)/shard_map/ppermute | solution.py:14
  246.1 0.0 collective-permute-done
  246.1 9.1 %collective-permute-done.1 = bf16[1,128,1792]{2,1,0:T(8,128)(2,1)S(1)} collective-permute-done((bf16[1,128,1792]{2,1,0:T(8,128)(2,1)S(1)}, bf16[1,128,1792]{2,1,0:T(8,128)(2,1)S(1)}, u32[]{:S(2)}, u32[]{:S(2)}) %collective-permute-start.1) | collective-permute-done | bytes 458784 | tf_op jit(solution)/shard_map/ppermute | solution.py:14
  255.2 0.8 copy.18
  256.0 0.8 copy.19
  (20 shorter events, 0.1 us)
Async XLA Ops:
  7.2 79.2 %copy-start = (bf16[1,1792,256]{2,1,0:T(8,128)(2,1)S(1)}, bf16[1,1792,256]{2,1,0:T(8,128)(2,1)}, u32[]{:S(2)}) copy-start(bf16[1,1792,256]{2,1,0:T(8,128)(2,1)} %param.14) | copy-start | bytes 2752516
  7.2 6.5 %copy-start.4 = (bf16[1,128,1792]{2,1,0:T(8,128)(2,1)S(1)}, bf16[1,128,1792]{2,1,0:T(8,128)(2,1)}, u32[]{:S(2)}) copy-start(bf16[1,128,1792]{2,1,0:T(8,128)(2,1)} %param.12) | copy-start | bytes 1376260
  51.9 4.5 %copy-start.5 = (bf16[1,128,1792]{2,1,0:T(8,128)(2,1)S(1)}, bf16[1,128,1792]{2,1,0:T(8,128)(2,1)}, u32[]{:S(2)}) copy-start(bf16[1,128,1792]{2,1,0:T(8,128)(2,1)} %param.13) | copy-start | bytes 1376260
  52.9 28.2 %all-to-all-start = ((bf16[16,16,1792]{2,1,0:T(8,128)(2,1)}), bf16[16,16,1792]{2,1,0:T(8,128)(2,1)S(1)}, u32[]{:S(2)}, u32[]{:S(2)}) async-start(bf16[16,16,1792]{2,1,0:T(8,128)(2,1)} %bitcast.84), calls=%async_computation | async-start | bytes 1835008 | tf_op jit(solution)/shard_map/all_to_all | solution.py:79
  82.1 28.8 %all-to-all-start.2 = ((bf16[16,16,1792]{2,1,0:T(8,128)(2,1)}), bf16[16,16,1792]{2,1,0:T(8,128)(2,1)}, u32[]{:S(2)}, u32[]{:S(2)}) async-start(bf16[16,16,1792]{2,1,0:T(8,128)(2,1)} %bitcast.85), calls=%async_computation.2 | async-start | bytes 1835008 | tf_op jit(solution)/shard_map/all_to_all | solution.py:93
  86.3 89.4 %all-reduce.3.cloned.1.call-start = ((), (), s32[]{:S(2)}) async-start(), calls=%async_computation.5 | async-start | bytes 2621440 | tf_op jit(solution)/shard_map/psum | solution.py:80
  86.4 1.2 copy-start.1
  88.7 22.2 %copy-start.3 = (bf16[1,256,1792]{2,1,0:T(8,128)(2,1)S(1)}, bf16[1,256,1792]{2,1,0:T(8,128)(2,1)}, u32[]{:S(2)}) copy-start(bf16[1,256,1792]{2,1,0:T(8,128)(2,1)} %param.16) | copy-start | bytes 2752516
  175.7 10.6 %copy-start.9 = (s32[2,1,1,2,16]{4,3,2,1,0:T(2,128)S(1)}, s32[2,1,1,2,16]{4,3,2,1,0:T(2,128)}, u32[]{:S(2)}) copy-start(s32[2,1,1,2,16]{4,3,2,1,0:T(2,128)} %param.18) | copy-start | bytes 772
  178.1 9.2 %copy-start.6 = (f32[16,16,256]{2,1,0:T(8,128)S(1)}, f32[16,16,256]{2,1,0:T(8,128)}, u32[]{:S(2)}) copy-start(f32[16,16,256]{2,1,0:T(8,128)} %get-tuple-element.7) | copy-start | bytes 786436
  178.1 9.2 %copy-start.7 = (f32[16,16,256]{2,1,0:T(8,128)S(1)}, f32[16,16,256]{2,1,0:T(8,128)}, u32[]{:S(2)}) copy-start(f32[16,16,256]{2,1,0:T(8,128)} %get-tuple-element.8) | copy-start | bytes 786436
  178.1 9.2 %copy-start.8 = (f32[16,16,256]{2,1,0:T(8,128)S(1)}, f32[16,16,256]{2,1,0:T(8,128)}, u32[]{:S(2)}) copy-start(f32[16,16,256]{2,1,0:T(8,128)} %get-tuple-element.9) | copy-start | bytes 786436
  178.1 33.5 %all-to-all-start.1 = ((bf16[16,16,1792]{2,1,0:T(8,128)(2,1)}), bf16[16,16,1792]{2,1,0:T(8,128)(2,1)S(1)}, u32[]{:S(2)}, u32[]{:S(2)}) async-start(bf16[16,16,1792]{2,1,0:T(8,128)(2,1)} %convolution_convert_fusion), calls=%async_computation.1 | async-start | bytes 1835008 | tf_op jit(solution)/shard_map/all_to_all | solution.py:82
  187.4 1.2 copy-start.2
  211.6 28.6 %all-to-all-start.4 = ((bf16[16,16,1792]{2,1,0:T(8,128)(2,1)}), bf16[16,16,1792]{2,1,0:T(8,128)(2,1)S(1)}, u32[]{:S(2)}, u32[]{:S(2)}) async-start(bf16[16,16,1792]{2,1,0:T(8,128)(2,1)} %fusion), calls=%async_computation.4 | async-start | bytes 1835008 | tf_op jit(solution)/shard_map/all_to_all | solution.py:109
  217.4 28.7 %collective-permute-start = (bf16[1,128,1792]{2,1,0:T(8,128)(2,1)}, bf16[1,128,1792]{2,1,0:T(8,128)(2,1)S(1)}, u32[]{:S(2)}, u32[]{:S(2)}) collective-permute-start(bf16[1,128,1792]{2,1,0:T(8,128)(2,1)} %convert_bitcast_fusion.1), channel_id=1, source_target_pairs={{0,32},{32,64},{64,96},{96,128},{128,160},{160,192},{192,224},{224... | collective-permute-start | bytes 1376264 | tf_op jit(solution)/shard_map/ppermute | solution.py:14
  241.6 13.6 %collective-permute-start.1 = (bf16[1,128,1792]{2,1,0:T(8,128)(2,1)S(1)}, bf16[1,128,1792]{2,1,0:T(8,128)(2,1)S(1)}, u32[]{:S(2)}, u32[]{:S(2)}) collective-permute-start(bf16[1,128,1792]{2,1,0:T(8,128)(2,1)S(1)} %convert_bitcast_fusion), channel_id=1, source_target_pairs={{0,480},{32,0},{64,32},{96,64},{128,96},{160,128},{192,160},{224,1... | collective-permute-start | bytes 1376264 | tf_op jit(solution)/shard_map/ppermute | solution.py:14
Sparse Core Ops, SparseCore 0:
  113.3 62.3 all-reduce.2
where the time goes:
time: 264 us
  waiting for transfers between devices  158 us (60%)
  blocking collectives  37.4 us (14%)
  starting transfers between devices  26.1 us (10%)
  between operations  14.3 us (5%)
  matrix products  11.1 us (4%)
  local copies, waits for them, and re-layouts  9.46 us (4%)
  other arithmetic  7.45 us (3%)
    psum x1, waiting for transfers between devices, per_device(): gate_fwd, up_fwd = lax.psum((gate_in(rows_fwd), up_in(rows_fwd)), 'dp')  62.5 us
    all_to_all x1, blocking collectives, per_device(): lax.all_to_all(sent_bwd, 'expert', split_axis=0, concat_axis=0, tiled=True)  37.4 us
    all_to_all x1, waiting for transfers between devices, per_device(): lax.all_to_all(sent_fwd, 'expert', split_axis=0, concat_axis=0, tiled=True)  23.9 us
    all_to_all x1, waiting for transfers between devices, per_device(): lax.all_to_all(jnp.einsum('jkf,fd->jkd', hidden, w_down, preferred_elemen...  21.7 us
    all_to_all x1, waiting for transfers between devices, per_device(): lax.all_to_all((first_term + jnp.einsum('jkf,df->jkd', grad_up, w_up, pre...  20.7 us
    all_to_all x1, waiting for transfers between devices, per_device(): lax.all_to_all(sent_grad, 'expert', split_axis=0, concat_axis=0, tiled=True)  20 us
    ppermute x2, waiting for transfers between devices, shifted(): lax.ppermute(shard, axis, [(i, (i + by) % peers) for i in range(peers)])  9.09 us
    all_to_all x1, starting transfers between devices, per_device(): lax.all_to_all(jnp.einsum('jkf,fd->jkd', hidden, w_down, preferred_elemen...  8.19 us
  transfers between devices with their start and end apart: 7, of which 6 were waited for; matrix products, arithmetic and copies ran while one was open for 4% of the time, Pallas kernels for 0%

commit v1 on v0

v1 whole, which is shorter than its diff:
```python
import functools

import jax
import jax.numpy as jnp
from jax import lax
from jax.experimental import pallas as pl
from jax.experimental.pallas import tpu as pltpu
from jax.sharding import PartitionSpec as P

MESH = pl.DeviceIdType.MESH
F32, BF16, I32 = jnp.float32, jnp.bfloat16, jnp.int32
ROUTED_SCALE = 2.5
EXPERTS = 2
CAP = 16
TOK = 128
CHIPS = 8
HALF = 4
FF = 256
ORDER = (1, 7, 2, 6, 3, 5, 4)


def dot(a, b, dims, precision=None):
    return lax.dot_general(a, b, ((dims[0], dims[1]), ((), ())), precision=precision, preferred_element_type=F32)


def column(row):
    wide = jnp.broadcast_to(row.astype(F32), (CAP, CAP))
    eye = lax.broadcasted_iota(I32, (CAP, CAP), 0) == lax.broadcasted_iota(I32, (CAP, CAP), 1)
    return jnp.sum(jnp.where(eye, wide, 0.0), axis=1, keepdims=True)


def picker(row):
    lanes = lax.broadcasted_iota(I32, (CAP, TOK), 1).astype(F32)
    return jnp.where(lanes == column(row), 1.0, 0.0)


def placer(row):
    tokens = lax.broadcasted_iota(I32, (TOK, CAP), 0)
    return jnp.where(tokens == jnp.broadcast_to(row, (TOK, CAP)), 1.0, 0.0)


def entry_weight(onehot, slot_row, affinity):
    picked = dot(onehot, affinity, ((1,), (1,)), lax.Precision.HIGHEST)
    slots = lax.broadcasted_iota(I32, (CAP, CHIPS), 1).astype(F32)
    chosen = jnp.sum(jnp.where(slots == column(slot_row), picked, 0.0), axis=1, keepdims=True)
    total = jnp.sum(picked, axis=1, keepdims=True)
    live = total > 0.0
    return jnp.where(live, ROUTED_SCALE * (chosen / jnp.where(live, total, 1.0)), 0.0)


def kernel(
    fin, sav, gra, wg_h, wu_h, wd_h, aff, lists, slots,
    out_f, out_b,
    vx, wgu, wd, snd, rcv, lst, nlst,
    part_f, part_b, part_g, xs_gu, xr_gu, xs_g, xr_g,
    hid, sib_s, sib_r, own, com_s, com_r, pip_s, pip_r, placed,
    load_sem, store_sem, dis_s, dis_r, fwd_s, fwd_r, dp_s, dp_r, ss_s, ss_r, co_s, co_r, pi_s, pi_r, li_s, li_r,
):
    p, x, d = lax.axis_index("pipe"), lax.axis_index("expert"), lax.axis_index("dp")
    pipes = lax.axis_size("pipe")
    z, c = lax.div(x, 2), lax.rem(x, 2)
    half = lax.div(z, HALF)
    sibling = (p, z * 2 + 1 - c, d)
    partner = (p, x, 1 - d)
    after = (lax.rem(p + 1, pipes), x, d)
    before = (lax.rem(p + pipes - 1, pipes), x, d)
    ahead = lambda k: lax.rem(z + k, CHIPS)
    behind = lambda k: lax.rem(z + CHIPS - k, CHIPS)
    at_chip = lambda zz: (p, zz * 2 + c, d)
    sent = []

    barrier = pltpu.get_barrier_semaphore()
    for peer in [at_chip(ahead(k)) for k in ORDER] + [sibling, partner, after, before]:
        pl.semaphore_signal(barrier, inc=1, device_id=peer, device_id_type=MESH)

    loads = [
        pltpu.make_async_copy(src, dst, load_sem.at[i])
        for i, (src, dst) in enumerate([
            (fin.at[0], vx.at[0]), (sav.at[0], vx.at[1]), (gra.at[0], vx.at[2]),
            (wg_h.at[0], wgu.at[:, pl.ds(0, FF)]), (wu_h.at[0], wgu.at[:, pl.ds(FF, FF)]), (wd_h.at[0], wd),
        ])
    ]
    for load in loads:
        load.start()

    def remote(src, dst, send_sem, recv_sem, device):
        return pltpu.make_async_remote_copy(
            src_ref=src, dst_ref=dst, send_sem=send_sem, recv_sem=recv_sem, device_id=device, device_id_type=MESH
        )

    def send(*args):
        copy = remote(*args)
        copy.start()
        sent.append(copy)

    rows = [[lists[f, 0, 0, pl.ds(e, 1), :] for e in range(EXPERTS)] for f in range(2)]
    slot_rows = [[slots[f, 0, 0, pl.ds(e, 1), :] for e in range(EXPERTS)] for f in range(2)]
    picks = [[picker(rows[f][e]) for e in range(EXPERTS)] for f in range(2)]
    weights = [[entry_weight(picks[f][e], slot_rows[f][e], aff[f, 0]) for e in range(EXPERTS)] for f in range(2)]
    lst[...] = jnp.zeros_like(lst)
    for f in range(2):
        lst[f, pl.ds(0, EXPERTS), pl.ds(0, CAP)] = lists[f, 0, 0]
    pick = [jnp.concatenate(picks[f], axis=0).astype(BF16) for f in range(2)]

    def gather(a):
        f = 0 if a == 0 else 1
        loads[a].wait()
        got = dot(pick[f], vx[a], ((1,), (0,)))
        for e in range(EXPERTS):
            block = got[e * CAP : (e + 1) * CAP]
            if a == 2:
                block = weights[1][e] * block
            snd[a, e] = block.astype(BF16)
        rcv[a, c * CHIPS + z] = snd[a, half]

    def dispatch(a):
        send(rcv.at[a, c * CHIPS + z], rcv.at[a, c * CHIPS + z], fwd_s.at[a, 0], fwd_r.at[a, 0], sibling)
        for k in ORDER:
            send(
                snd.at[a, lax.div(ahead(k), HALF)], rcv.at[a, c * CHIPS + z],
                dis_s.at[a, k], dis_r.at[a, k], at_chip(ahead(k)),
            )

    def forward(a):
        for k in ORDER:
            slot = c * CHIPS + behind(k)
            remote(snd.at[a, 0], rcv.at[a, slot], dis_s.at[a, k], dis_r.at[a, k], sibling).wait_recv()
            send(rcv.at[a, slot], rcv.at[a, slot], fwd_s.at[a, k], fwd_r.at[a, k], sibling)
        for k in (0,) + ORDER:
            slot = (1 - c) * CHIPS + behind(k)
            remote(snd.at[a, 0], rcv.at[a, slot], fwd_s.at[a, k], fwd_r.at[a, k], sibling).wait_recv()

    def all_rows(a):
        return rcv[a].reshape(2 * CHIPS * CAP, rcv.shape[-1])

    gather(0)
    pl.semaphore_wait(barrier, len(ORDER) + 4)
    dispatch(0)
    gather(1)
    dispatch(1)
    gather(2)
    dispatch(2)
    send(lst.at[0], nlst.at[0], li_s.at[0], li_r.at[0], after)
    send(lst.at[1], nlst.at[1], li_s.at[1], li_r.at[1], before)
    for load in loads[3:]:
        load.wait()

    def exchange_gu(f):
        part = part_f if f == 0 else part_b
        got = dot(all_rows(f), wgu[...], ((1,), (0,)))
        part[...] = got
        xs_gu[f] = got.astype(BF16)
        send(xs_gu.at[f], xr_gu.at[f], dp_s.at[f], dp_r.at[f], partner)

    def joined_gu(f):
        part = part_f if f == 0 else part_b
        remote(xs_gu.at[f], xr_gu.at[f], dp_s.at[f], dp_r.at[f], partner).wait_recv()
        total = part[...] + xr_gu[f].astype(F32)
        return total[:, :FF], total[:, FF:]

    def back(f, hidden):
        hid[f, :, :, pl.ds(0, hidden.shape[-1])] = hidden.reshape(2, CHIPS * CAP, hidden.shape[-1])

    def product(f, core):
        if f == 0:
            return dot(hid[0, core, :, pl.ds(0, FF)], wd[...], ((1,), (0,)))
        return dot(hid[1, core], wgu[...], ((1,), (1,)))

    def to_sibling(f):
        sib_s[f] = product(f, 1 - c).astype(BF16).reshape(CHIPS, CAP, wd.shape[-1])
        send(sib_s.at[f], sib_r.at[f], ss_s.at[f], ss_r.at[f], sibling)
        own[f] = product(f, c).reshape(CHIPS, CAP, wd.shape[-1])

    def combine(f):
        remote(sib_s.at[f], sib_r.at[f], ss_s.at[f], ss_r.at[f], sibling).wait_recv()
        com_s[f] = (own[f] + sib_r[f].astype(F32)).astype(BF16)
        com_r[f, z] = com_s[f, z]
        for k in ORDER:
            send(com_s.at[f, ahead(k)], com_r.at[f, z], co_s.at[f, k], co_r.at[f, k], at_chip(ahead(k)))

    def hand_on(f):
        for k in ORDER:
            remote(com_s.at[f, 0], com_r.at[f, behind(k)], co_s.at[f, k], co_r.at[f, k], sibling).wait_recv()
        for e in range(EXPERTS):
            total = jnp.sum(com_r[f, pl.ds(e * HALF, HALF)].astype(F32), axis=0)
            if f == 0:
                total = weights[0][e] * total
            pip_s[f, e] = total.astype(BF16)
        send(pip_s.at[f], pip_r.at[f], pi_s.at[f], pi_r.at[f], after if f == 0 else before)

    def place(f):
        toward = after if f == 0 else before
        remote(lst.at[f], nlst.at[f], li_s.at[f], li_r.at[f], toward).wait_recv()
        remote(pip_s.at[f], pip_r.at[f], pi_s.at[f], pi_r.at[f], toward).wait_recv()
        total = None
        for e in range(EXPERTS):
            spot = placer(nlst[f, pl.ds(e, 1), pl.ds(0, CAP)]).astype(BF16)
            term = dot(spot, pip_r[f, e], ((1,), (0,)))
            total = term if total is None else total + term
        placed[f] = total.astype(BF16)
        copy = pltpu.make_async_copy(placed.at[f], (out_f if f == 0 else out_b).at[0], store_sem.at[f])
        copy.start()
        return copy

    forward(0)
    exchange_gu(0)
    gate, up = joined_gu(0)
    back(0, (gate * jax.nn.sigmoid(gate) * up).astype(BF16))
    to_sibling(0)
    forward(1)
    combine(0)
    exchange_gu(1)
    forward(2)
    part_g[...] = dot(all_rows(2), wd[...], ((1,), (1,)))
    xs_g[...] = part_g[...].astype(BF16)
    send(xs_g, xr_g, dp_s.at[2], dp_r.at[2], partner)
    gate, up = joined_gu(1)
    sg = jax.nn.sigmoid(gate)
    remote(xs_g, xr_g, dp_s.at[2], dp_r.at[2], partner).wait_recv()
    grad = part_g[...] + xr_g[...].astype(F32)
    grad_gate = (grad * up * sg * (1.0 + gate * (1.0 - sg))).astype(BF16)
    grad_up = (grad * gate * sg).astype(BF16)
    back(1, jnp.concatenate([grad_gate, grad_up], axis=1))
    to_sibling(1)
    hand_on(0)
    combine(1)
    first = place(0)
    hand_on(1)
    second = place(1)
    for copy in sent:
        copy.wait_send()
    first.wait()
    second.wait()


def per_device(forward_input, saved_input, output_grad, gate_proj, up_proj, down_proj, affinity, token_lists, slot_ids):
    width = forward_input.shape[-1]
    whole = pl.BlockSpec(memory_space=pl.ANY)
    small = pl.BlockSpec(memory_space=pltpu.VMEM)
    blocks = 2 * CHIPS
    entries = blocks * CAP
    dma = pltpu.SemaphoreType.DMA
    return pl.pallas_call(
        kernel,
        out_shape=(jax.ShapeDtypeStruct((1, TOK, width), BF16),) * 2,
        in_specs=[whole] * 6 + [small] * 3,
        out_specs=(whole, whole),
        scratch_shapes=[
            pltpu.VMEM((3, TOK, width), BF16),
            pltpu.VMEM((width, 2 * FF), BF16),
            pltpu.VMEM((FF, width), BF16),
            pltpu.VMEM((3, EXPERTS, CAP, width), BF16),
            pltpu.VMEM((3, blocks, CAP, width), BF16),
            pltpu.VMEM((2, 8, 128), I32),
            pltpu.VMEM((2, 8, 128), I32),
            pltpu.VMEM((entries, 2 * FF), F32),
            pltpu.VMEM((entries, 2 * FF), F32),
            pltpu.VMEM((entries, FF), F32),
            pltpu.VMEM((2, entries, 2 * FF), BF16),
            pltpu.VMEM((2, entries, 2 * FF), BF16),
            pltpu.VMEM((entries, FF), BF16),
            pltpu.VMEM((entries, FF), BF16),
            pltpu.VMEM((2, 2, CHIPS * CAP, 2 * FF), BF16),
            pltpu.VMEM((2, CHIPS, CAP, width), BF16),
            pltpu.VMEM((2, CHIPS, CAP, width), BF16),
            pltpu.VMEM((2, CHIPS, CAP, width), F32),
            pltpu.VMEM((2, CHIPS, CAP, width), BF16),
            pltpu.VMEM((2, CHIPS, CAP, width), BF16),
            pltpu.VMEM((2, EXPERTS, CAP, width), BF16),
            pltpu.VMEM((2, EXPERTS, CAP, width), BF16),
            pltpu.VMEM((2, TOK, width), BF16),
            dma((6,)), dma((2,)),
            dma((3, CHIPS)), dma((3, CHIPS)), dma((3, CHIPS)), dma((3, CHIPS)),
            dma((3,)), dma((3,)), dma((2,)), dma((2,)),
            dma((2, CHIPS)), dma((2, CHIPS)), dma((2,)), dma((2,)), dma((2,)), dma((2,)),
        ],
        compiler_params=pltpu.CompilerParams(
            collective_id=0, has_side_effects=True, vmem_limit_bytes=48 * 1024 * 1024
        ),
        cost_estimate=pl.CostEstimate(flops=2_000_000_000, bytes_accessed=6_000_000, transcendentals=262_144),
    )(
        forward_input, saved_input, output_grad, gate_proj, up_proj, down_proj,
        jnp.swapaxes(affinity, 2, 3), token_lists, slot_ids,
    )


def solution(mesh):
    in_specs = (
        P("pipe", "expert", "dp"),
        P("pipe", "expert", "dp"),
        P("pipe", "expert", "dp"),
        P("pipe", "dp", "expert"),
        P("pipe", "dp", "expert"),
        P("pipe", "expert", "dp"),
        P(None, "pipe", "expert", None),
        P(None, "pipe", "expert", None, None),
        P(None, "pipe", "expert", None, None),
    )
    out_specs = (P("pipe", "expert", "dp"), P("pipe", "expert", "dp"))
    return jax.shard_map(
        per_device, mesh=mesh, in_specs=in_specs, out_specs=out_specs, check_vma=False
    )
```

time: 264 us -> 85.9 us (0.33)
  the two profiles are of different devices: /device:TPU:1 before, /device:TPU:154 now
where the time goes in v1:
time: 85.9 us; the launch traced here: 85.4 us
  Pallas kernels  74.6 us (87%)
  local copies, waits for them, and re-layouts  10.2 us (12%)
    pallas_call x1, Pallas kernels, per_device(): pl.pallas_call(kernel, out_shape=(jax.ShapeDtypeStruct((1, TOK, width), B...  74.6 us
    unnamed x20, local copies, waits for them, and re-layouts  10.2 us

profile of v1, /device:TPU:154, one launch (start us, length us, event | category | flops | bytes accessed | tf_op | source)
XLA Modules:
  0.0 85.4 jit_solution(261640330285539356)
XLA Ops:
  0.6 0.0 copy-start
  0.6 1.2 %copy-done = bf16[1,1792,256]{2,1,0:T(8,128)(2,1)S(1)} copy-done((bf16[1,1792,256]{2,1,0:T(8,128)(2,1)S(1)}, bf16[1,1792,256]{2,1,0:T(8,128)(2,1)}, u32[]{:S(2)}) %copy-start) | copy-done | bytes 917528
  1.8 0.0 copy-start.1
  1.8 1.2 %copy-done.1 = bf16[1,1792,256]{2,1,0:T(8,128)(2,1)S(1)} copy-done((bf16[1,1792,256]{2,1,0:T(8,128)(2,1)S(1)}, bf16[1,1792,256]{2,1,0:T(8,128)(2,1)}, u32[]{:S(2)}) %copy-start.1) | copy-done | bytes 917528
  3.0 0.0 copy-start.2
  3.0 1.2 %copy-done.2 = bf16[1,256,1792]{2,1,0:T(8,128)(2,1)S(1)} copy-done((bf16[1,256,1792]{2,1,0:T(8,128)(2,1)S(1)}, bf16[1,256,1792]{2,1,0:T(8,128)(2,1)}, u32[]{:S(2)}) %copy-start.2) | copy-done | bytes 917528
  4.2 0.0 copy-start.3
  4.2 1.0 %copy-done.3 = bf16[1,128,1792]{2,1,0:T(8,128)(2,1)S(1)} copy-done((bf16[1,128,1792]{2,1,0:T(8,128)(2,1)S(1)}, bf16[1,128,1792]{2,1,0:T(8,128)(2,1)}, u32[]{:S(2)}) %copy-start.3) | copy-done | bytes 458776
  5.2 0.0 copy-start.4
  5.2 1.0 %copy-done.4 = bf16[1,128,1792]{2,1,0:T(8,128)(2,1)S(1)} copy-done((bf16[1,128,1792]{2,1,0:T(8,128)(2,1)S(1)}, bf16[1,128,1792]{2,1,0:T(8,128)(2,1)}, u32[]{:S(2)}) %copy-start.4) | copy-done | bytes 458776
  6.2 0.0 copy-start.5
  6.2 1.0 %copy-done.5 = bf16[1,128,1792]{2,1,0:T(8,128)(2,1)S(1)} copy-done((bf16[1,128,1792]{2,1,0:T(8,128)(2,1)S(1)}, bf16[1,128,1792]{2,1,0:T(8,128)(2,1)}, u32[]{:S(2)}) %copy-start.5) | copy-done | bytes 458776
  7.2 0.0 copy-start.6
  7.2 0.7 copy-done.6
  7.9 0.0 copy-start.7
  7.9 0.7 copy-done.7
  8.6 0.0 copy-start.8
  8.6 0.7 copy-done.8
  9.3 74.6 %shard_map.104 = (bf16[1,128,1792]{2,1,0:T(8,128)(2,1)S(1)}, bf16[1,128,1792]{2,1,0:T(8,128)(2,1)S(1)}) custom-call(bf16[1,128,1792]{2,1,0:T(8,128)(2,1)S(1)} %copy-done.3, bf16[1,128,1792]{2,1,0:T(8,128)(2,1)S(1)} %copy-done.4, bf16[1,128,1792]{2,1,0:T(8,128)(2,1)S(1)} %copy-done.5, bf16[1,1792,256]{2,1,0:T(8,128)(2,1)S(1)} %copy-done, ...), custom_call_target="tpu_custom_call" | custom-call | flops 2000000000 | bytes 6000000 | tf_op jit(solution)/shard_map/pallas_call | solution.py:243
  83.9 0.8 copy.13
  84.6 0.8 copy.14
Async XLA Ops:
  0.6 1.2 %copy-start = (bf16[1,1792,256]{2,1,0:T(8,128)(2,1)S(1)}, bf16[1,1792,256]{2,1,0:T(8,128)(2,1)}, u32[]{:S(2)}) copy-start(bf16[1,1792,256]{2,1,0:T(8,128)(2,1)} %wg_h.1) | copy-start | bytes 2752516
  1.8 1.2 %copy-start.1 = (bf16[1,1792,256]{2,1,0:T(8,128)(2,1)S(1)}, bf16[1,1792,256]{2,1,0:T(8,128)(2,1)}, u32[]{:S(2)}) copy-start(bf16[1,1792,256]{2,1,0:T(8,128)(2,1)} %wu_h.1) | copy-start | bytes 2752516
  3.0 1.2 %copy-start.2 = (bf16[1,256,1792]{2,1,0:T(8,128)(2,1)S(1)}, bf16[1,256,1792]{2,1,0:T(8,128)(2,1)}, u32[]{:S(2)}) copy-start(bf16[1,256,1792]{2,1,0:T(8,128)(2,1)} %wd_h.1) | copy-start | bytes 2752516
  4.2 1.0 %copy-start.3 = (bf16[1,128,1792]{2,1,0:T(8,128)(2,1)S(1)}, bf16[1,128,1792]{2,1,0:T(8,128)(2,1)}, u32[]{:S(2)}) copy-start(bf16[1,128,1792]{2,1,0:T(8,128)(2,1)} %fin.1) | copy-start | bytes 1376260
  5.2 1.0 %copy-start.4 = (bf16[1,128,1792]{2,1,0:T(8,128)(2,1)S(1)}, bf16[1,128,1792]{2,1,0:T(8,128)(2,1)}, u32[]{:S(2)}) copy-start(bf16[1,128,1792]{2,1,0:T(8,128)(2,1)} %sav.1) | copy-start | bytes 1376260
  6.2 1.0 %copy-start.5 = (bf16[1,128,1792]{2,1,0:T(8,128)(2,1)S(1)}, bf16[1,128,1792]{2,1,0:T(8,128)(2,1)}, u32[]{:S(2)}) copy-start(bf16[1,128,1792]{2,1,0:T(8,128)(2,1)} %gra.1) | copy-start | bytes 1376260
  7.2 0.7 copy-start.6
  7.9 0.7 copy-start.7
  8.6 0.7 copy-start.8

commit v2 on v1

--- a/solution.py
+++ b/solution.py
@@ -16,7 +16,9 @@
 CHIPS = 8
 HALF = 4
 FF = 256
-ORDER = (1, 7, 2, 6, 3, 5, 4)
+VMEM_LIMIT = 62 * 1024 * 1024
+STEPS = (3, 2, 1)
+PEERS = (1, 2, 3, 4, -1, -2, -3)
 
 
 def dot(a, b, dims, precision=None):
@@ -49,12 +51,12 @@
 
 
 def kernel(
-    fin, sav, gra, wg_h, wu_h, wd_h, aff, lists, slots,
+    fin, sav, gra, wg_h, wu_h, wd_h, aff_h, lists_h, slots_h,
     out_f, out_b,
-    vx, wgu, wd, snd, rcv, lst, nlst,
+    aff, lists, slots, vx, wgu, wd, snd, rcv, lst, nlst,
     part_f, part_b, part_g, xs_gu, xr_gu, xs_g, xr_g,
-    hid, sib_s, sib_r, own, com_s, com_r, pip_s, pip_r, placed,
-    load_sem, store_sem, dis_s, dis_r, fwd_s, fwd_r, dp_s, dp_r, ss_s, ss_r, co_s, co_r, pi_s, pi_r, li_s, li_r,
+    hid, sib_s, sib_r, own, mate_s, mate_r, com_s, com_r, pip_s, pip_r, placed,
+    load_sem, store_sem, dis_s, dis_r, fwd_s, fwd_r, dp_s, dp_r, ss_s, ss_r, ma_s, ma_r, co_s, co_r, pi_s, pi_r, li_s, li_r,
 ):
     p, x, d = lax.axis_index("pipe"), lax.axis_index("expert"), lax.axis_index("dp")
     pipes = lax.axis_size("pipe")
@@ -64,13 +66,14 @@
     partner = (p, x, 1 - d)
     after = (lax.rem(p + 1, pipes), x, d)
     before = (lax.rem(p + pipes - 1, pipes), x, d)
-    ahead = lambda k: lax.rem(z + k, CHIPS)
-    behind = lambda k: lax.rem(z + CHIPS - k, CHIPS)
-    at_chip = lambda zz: (p, zz * 2 + c, d)
+    toward = 2 * lax.rem(z, 2) - 1
+    chip = lambda k: lax.rem(z + CHIPS + k * toward, CHIPS)
+    at_chip = lambda k: (p, chip(k) * 2 + c, d)
+    goal = {1: 1, 2: -2, 3: 3}
     sent = []
 
     barrier = pltpu.get_barrier_semaphore()
-    for peer in [at_chip(ahead(k)) for k in ORDER] + [sibling, partner, after, before]:
+    for peer in [at_chip(k) for k in PEERS] + [sibling, partner, after, before]:
         pl.semaphore_signal(barrier, inc=1, device_id=peer, device_id_type=MESH)
 
     loads = [
@@ -80,8 +83,12 @@
             (wg_h.at[0], wgu.at[:, pl.ds(0, FF)]), (wu_h.at[0], wgu.at[:, pl.ds(FF, FF)]), (wd_h.at[0], wd),
         ])
     ]
-    for load in loads:
-        load.start()
+    loads += [
+        pltpu.make_async_copy(src, dst, load_sem.at[6 + i])
+        for i, (src, dst) in enumerate([(lists_h, lists), (slots_h, slots), (aff_h, aff)])
+    ]
+    for i in (6, 7, 8, 0, 1, 2, 3, 4, 5):
+        loads[i].start()
 
     def remote(src, dst, send_sem, recv_sem, device):
         return pltpu.make_async_remote_copy(
@@ -93,6 +100,8 @@
         copy.start()
         sent.append(copy)
 
+    for i in (6, 7, 8):
+        loads[i].wait()
     rows = [[lists[f, 0, 0, pl.ds(e, 1), :] for e in range(EXPERTS)] for f in range(2)]
     slot_rows = [[slots[f, 0, 0, pl.ds(e, 1), :] for e in range(EXPERTS)] for f in range(2)]
     picks = [[picker(rows[f][e]) for e in range(EXPERTS)] for f in range(2)]
@@ -113,36 +122,52 @@
             snd[a, e] = block.astype(BF16)
         rcv[a, c * CHIPS + z] = snd[a, half]
 
+    def slot_of(k, core=None):
+        return (c if core is None else core) * CHIPS + chip(k)
+
     def dispatch(a):
-        send(rcv.at[a, c * CHIPS + z], rcv.at[a, c * CHIPS + z], fwd_s.at[a, 0], fwd_r.at[a, 0], sibling)
-        for k in ORDER:
+        for k in STEPS:
             send(
-                snd.at[a, lax.div(ahead(k), HALF)], rcv.at[a, c * CHIPS + z],
-                dis_s.at[a, k], dis_r.at[a, k], at_chip(ahead(k)),
+                snd.at[a, lax.div(chip(goal[k]), HALF)], rcv.at[a, slot_of(0)],
+                dis_s.at[a, k], dis_r.at[a, k], at_chip(goal[k]),
             )
-
-    def forward(a):
-        for k in ORDER:
-            slot = c * CHIPS + behind(k)
-            remote(snd.at[a, 0], rcv.at[a, slot], dis_s.at[a, k], dis_r.at[a, k], sibling).wait_recv()
-            send(rcv.at[a, slot], rcv.at[a, slot], fwd_s.at[a, k], fwd_r.at[a, k], sibling)
-        for k in (0,) + ORDER:
-            slot = (1 - c) * CHIPS + behind(k)
-            remote(snd.at[a, 0], rcv.at[a, slot], fwd_s.at[a, k], fwd_r.at[a, k], sibling).wait_recv()
+        send(snd.at[a, half], rcv.at[a, slot_of(0)], dis_s.at[a, 0], dis_r.at[a, 0], at_chip(-1))
+        share(a, 0, 0)
+
+    def share(a, k, i):
+        send(rcv.at[a, slot_of(k)], rcv.at[a, slot_of(k)], fwd_s.at[a, i], fwd_r.at[a, i], sibling)
+
+    def arrived(a, k, i, sems=None, core=None):
+        remote(snd.at[a, 0], rcv.at[a, slot_of(k, core)], dis_s.at[a, i], (dis_r if sems is None else sems).at[a, i], sibling).wait_recv()
+
+    def relay(a):
+        for k in (1, 2, 3):
+            arrived(a, k, k)
+            send(rcv.at[a, slot_of(k)], rcv.at[a, slot_of(k)], dis_s.at[a, 4 + k], dis_r.at[a, 4 + k], at_chip(-1))
+            share(a, k, k)
+
+    def collect(a):
+        arrived(a, -1, 0)
+        share(a, -1, 4)
+        for k in (1, 2, 3):
+            arrived(a, -1 - k, 4 + k)
+            share(a, -1 - k, 4 + k)
+        for k, i in ((0, 0), (1, 1), (2, 2), (3, 3), (-1, 4), (-2, 5), (-3, 6), (-4, 7)):
+            arrived(a, k, i, fwd_r, 1 - c)
 
     def all_rows(a):
         return rcv[a].reshape(2 * CHIPS * CAP, rcv.shape[-1])
 
     gather(0)
-    pl.semaphore_wait(barrier, len(ORDER) + 4)
+    gather(1)
+    pl.semaphore_wait(barrier, len(PEERS) + 4)
     dispatch(0)
-    gather(1)
     dispatch(1)
     gather(2)
     dispatch(2)
     send(lst.at[0], nlst.at[0], li_s.at[0], li_r.at[0], after)
     send(lst.at[1], nlst.at[1], li_s.at[1], li_r.at[1], before)
-    for load in loads[3:]:
+    for load in loads[3:6]:
         load.wait()
 
     def exchange_gu(f):
@@ -171,27 +196,40 @@
         send(sib_s.at[f], sib_r.at[f], ss_s.at[f], ss_r.at[f], sibling)
         own[f] = product(f, c).reshape(CHIPS, CAP, wd.shape[-1])
 
+    def gathered(f, k):
+        return own[f, chip(k)] + sib_r[f, chip(k)].astype(F32)
+
+    def to_mate(f):
+        remote(sib_s.at[f], sib_r.at[f], ss_s.at[f], ss_r.at[f], sibling).wait_recv()
+        for k in STEPS + (0,):
+            mate_s[f, k] = gathered(f, -1 - k).astype(BF16)
+            send(mate_s.at[f, k], mate_r.at[f, k], ma_s.at[f, k], ma_r.at[f, k], at_chip(-1))
+
+    def from_mate(f, k):
+        remote(mate_s.at[f, k], mate_r.at[f, k], ma_s.at[f, k], ma_r.at[f, k], sibling).wait_recv()
+        return (gathered(f, k) + mate_r[f, k].astype(F32)).astype(BF16)
+
     def combine(f):
-        remote(sib_s.at[f], sib_r.at[f], ss_s.at[f], ss_r.at[f], sibling).wait_recv()
-        com_s[f] = (own[f] + sib_r[f].astype(F32)).astype(BF16)
-        com_r[f, z] = com_s[f, z]
-        for k in ORDER:
-            send(com_s.at[f, ahead(k)], com_r.at[f, z], co_s.at[f, k], co_r.at[f, k], at_chip(ahead(k)))
+        pair = lax.div(z, 2)
+        for k in STEPS:
+            com_s[f, k] = from_mate(f, k)
+            send(com_s.at[f, k], com_r.at[f, pair], co_s.at[f, k], co_r.at[f, k], at_chip(k))
+        com_r[f, pair] = from_mate(f, 0)
 
     def hand_on(f):
-        for k in ORDER:
-            remote(com_s.at[f, 0], com_r.at[f, behind(k)], co_s.at[f, k], co_r.at[f, k], sibling).wait_recv()
+        for k in (1, 2, 3):
+            source = lax.div(chip(goal[k]), 2)
+            remote(com_s.at[f, k], com_r.at[f, source], co_s.at[f, k], co_r.at[f, k], sibling).wait_recv()
         for e in range(EXPERTS):
-            total = jnp.sum(com_r[f, pl.ds(e * HALF, HALF)].astype(F32), axis=0)
+            total = com_r[f, 2 * e].astype(F32) + com_r[f, 2 * e + 1].astype(F32)
             if f == 0:
                 total = weights[0][e] * total
             pip_s[f, e] = total.astype(BF16)
         send(pip_s.at[f], pip_r.at[f], pi_s.at[f], pi_r.at[f], after if f == 0 else before)
 
     def place(f):
-        toward = after if f == 0 else before
-        remote(lst.at[f], nlst.at[f], li_s.at[f], li_r.at[f], toward).wait_recv()
-        remote(pip_s.at[f], pip_r.at[f], pi_s.at[f], pi_r.at[f], toward).wait_recv()
+        remote(lst.at[f], nlst.at[f], li_s.at[f], li_r.at[f], after).wait_recv()
+        remote(pip_s.at[f], pip_r.at[f], pi_s.at[f], pi_r.at[f], after).wait_recv()
         total = None
         for e in range(EXPERTS):
             spot = placer(nlst[f, pl.ds(e, 1), pl.ds(0, CAP)]).astype(BF16)
@@ -202,18 +240,21 @@
         copy.start()
         return copy
 
-    forward(0)
+    relay(0)
+    relay(1)
+    collect(0)
     exchange_gu(0)
+    relay(2)
+    collect(1)
+    exchange_gu(1)
     gate, up = joined_gu(0)
     back(0, (gate * jax.nn.sigmoid(gate) * up).astype(BF16))
     to_sibling(0)
-    forward(1)
-    combine(0)
-    exchange_gu(1)
-    forward(2)
+    collect(2)
     part_g[...] = dot(all_rows(2), wd[...], ((1,), (1,)))
     xs_g[...] = part_g[...].astype(BF16)
     send(xs_g, xr_g, dp_s.at[2], dp_r.at[2], partner)
+    to_mate(0)
     gate, up = joined_gu(1)
     sg = jax.nn.sigmoid(gate)
     remote(xs_g, xr_g, dp_s.at[2], dp_r.at[2], partner).wait_recv()
@@ -222,6 +263,8 @@
     grad_up = (grad * gate * sg).astype(BF16)
     back(1, jnp.concatenate([grad_gate, grad_up], axis=1))
     to_sibling(1)
+    combine(0)
+    to_mate(1)
     hand_on(0)
     combine(1)
     first = place(0)
@@ -235,17 +278,19 @@
 
 def per_device(forward_input, saved_input, output_grad, gate_proj, up_proj, down_proj, affinity, token_lists, slot_ids):
     width = forward_input.shape[-1]
-    whole = pl.BlockSpec(memory_space=pl.ANY)
-    small = pl.BlockSpec(memory_space=pltpu.VMEM)
+    whole = pl.BlockSpec(memory_space=pltpu.HBM)
     blocks = 2 * CHIPS
     entries = blocks * CAP
     dma = pltpu.SemaphoreType.DMA
     return pl.pallas_call(
         kernel,
         out_shape=(jax.ShapeDtypeStruct((1, TOK, width), BF16),) * 2,
-        in_specs=[whole] * 6 + [small] * 3,
+        in_specs=[whole] * 9,
         out_specs=(whole, whole),
         scratch_shapes=[
+            pltpu.VMEM((2, 1, CHIPS, TOK), F32),
+            pltpu.VMEM((2, 1, 1, EXPERTS, CAP), I32),
+            pltpu.VMEM((2, 1, 1, EXPERTS, CAP), I32),
             pltpu.VMEM((3, TOK, width), BF16),
             pltpu.VMEM((width, 2 * FF), BF16),
             pltpu.VMEM((FF, width), BF16),
@@ -264,18 +309,20 @@
             pltpu.VMEM((2, CHIPS, CAP, width), BF16),
             pltpu.VMEM((2, CHIPS, CAP, width), BF16),
             pltpu.VMEM((2, CHIPS, CAP, width), F32),
-            pltpu.VMEM((2, CHIPS, CAP, width), BF16),
-            pltpu.VMEM((2, CHIPS, CAP, width), BF16),
+            pltpu.VMEM((2, 4, CAP, width), BF16),
+            pltpu.VMEM((2, 4, CAP, width), BF16),
+            pltpu.VMEM((2, 4, CAP, width), BF16),
+            pltpu.VMEM((2, 4, CAP, width), BF16),
             pltpu.VMEM((2, EXPERTS, CAP, width), BF16),
             pltpu.VMEM((2, EXPERTS, CAP, width), BF16),
             pltpu.VMEM((2, TOK, width), BF16),
-            dma((6,)), dma((2,)),
+            dma((9,)), dma((2,)),
             dma((3, CHIPS)), dma((3, CHIPS)), dma((3, CHIPS)), dma((3, CHIPS)),
-            dma((3,)), dma((3,)), dma((2,)), dma((2,)),
-            dma((2, CHIPS)), dma((2, CHIPS)), dma((2,)), dma((2,)), dma((2,)), dma((2,)),
+            dma((3,)), dma((3,)), dma((2,)), dma((2,)), dma((2, 4)), dma((2, 4)),
+            dma((2, 4)), dma((2, 4)), dma((2,)), dma((2,)), dma((2,)), dma((2,)),
         ],
         compiler_params=pltpu.CompilerParams(
-            collective_id=0, has_side_effects=True, vmem_limit_bytes=48 * 1024 * 1024
+            collective_id=0, has_side_effects=True, vmem_limit_bytes=VMEM_LIMIT
         ),
         cost_estimate=pl.CostEstimate(flops=2_000_000_000, bytes_accessed=6_000_000, transcendentals=262_144),
     )(

time: 85.9 us -> 74.7 us (0.87)
  the two profiles are of different devices: /device:TPU:154 before, /device:TPU:26 now
where the time goes in v2:
time: 74.7 us; the launch traced here: 74.6 us
  Pallas kernels  71.3 us (95%)
  local copies, waits for them, and re-layouts  2.64 us (4%)
    pallas_call x1, Pallas kernels, per_device(): pl.pallas_call(kernel, out_shape=(jax.ShapeDtypeStruct((1, TOK, width), B...  71.3 us
    unnamed x4, local copies, waits for them, and re-layouts  2.64 us

profile of v2, /device:TPU:26, one launch (start us, length us, event | category | flops | bytes accessed | tf_op | source)
XLA Modules:
  0.0 74.6 jit_solution(3094308963381799126)
XLA Ops:
  0.6 71.3 %shard_map.104 = (bf16[1,128,1792]{2,1,0:T(8,128)(2,1)}, bf16[1,128,1792]{2,1,0:T(8,128)(2,1)}) custom-call(bf16[1,128,1792]{2,1,0:T(8,128)(2,1)} %fin.1, bf16[1,128,1792]{2,1,0:T(8,128)(2,1)} %sav.1, bf16[1,128,1792]{2,1,0:T(8,128)(2,1)} %gra.1, bf16[1,1792,256]{2,1,0:T(8,128)(2,1)} %wg_h.1, bf16[1,1792,256]{2,1,0:T(8,128)(2,1)} %wu_h.1, ...), custom_call_target="tpu_custom_call" | custom-call | flops 2000000000 | bytes 6000000 | tf_op jit(solution)/shard_map/pallas_call | solution.py:285
  71.9 0.0 copy-start
  72.0 1.9 %copy.13 = bf16[1,128,1792]{2,1,0:T(8,128)(2,1)} copy(bf16[1,128,1792]{2,1,0:T(8,128)(2,1)} %get-tuple-element.4) | data formatting | bytes 917504
  73.8 0.0 copy-done
  73.8 0.8 %copy.14 = bf16[1,128,1792]{2,1,0:T(8,128)(2,1)} copy(bf16[1,128,1792]{2,1,0:T(8,128)(2,1)S(1)} %copy-done) | data formatting | bytes 917504
Async XLA Ops:
  71.9 1.9 %copy-start = (bf16[1,128,1792]{2,1,0:T(8,128)(2,1)S(1)}, bf16[1,128,1792]{2,1,0:T(8,128)(2,1)}, u32[]{:S(2)}) copy-start(bf16[1,128,1792]{2,1,0:T(8,128)(2,1)} %get-tuple-element.5) | copy-start | bytes 1376260

commit v3 on v2

v3 whole, which is shorter than its diff:
```python
import functools

import jax
import jax.numpy as jnp
from jax import lax
from jax.experimental import pallas as pl
from jax.experimental.pallas import tpu as pltpu
from jax.sharding import PartitionSpec as P

MESH = pl.DeviceIdType.MESH
F32, BF16, I32 = jnp.float32, jnp.bfloat16, jnp.int32
ROUTED_SCALE = 2.5
EXPERTS = 2
CAP = 16
TOK = 128
CHIPS = 8
HALF = 4
FF = 256
VMEM_LIMIT = 62 * 1024 * 1024
STEPS = (3, 2, 1)
PEERS = (1, 2, 3, 4, -1, -2, -3)
EARLY = 5
SHARES = ((5, 8), (0, 5))
PARTS = ((0, EARLY), (EARLY, CHIPS))
CUTS = (((0, 1792),), ((0, 1792),))
MOST = 2


def dot(a, b, dims, precision=None):
    return lax.dot_general(a, b, ((dims[0], dims[1]), ((), ())), precision=precision, preferred_element_type=F32)


def column(row):
    wide = jnp.broadcast_to(row.astype(F32), (CAP, CAP))
    eye = lax.broadcasted_iota(I32, (CAP, CAP), 0) == lax.broadcasted_iota(I32, (CAP, CAP), 1)
    return jnp.sum(jnp.where(eye, wide, 0.0), axis=1, keepdims=True)


def picker(row):
    lanes = lax.broadcasted_iota(I32, (CAP, TOK), 1).astype(F32)
    return jnp.where(lanes == column(row), 1.0, 0.0)


def placer(row):
    tokens = lax.broadcasted_iota(I32, (TOK, CAP), 0)
    return jnp.where(tokens == jnp.broadcast_to(row, (TOK, CAP)), 1.0, 0.0)


def entry_weight(onehot, slot_row, affinity):
    picked = dot(onehot, affinity, ((1,), (1,)), lax.Precision.HIGHEST)
    slots = lax.broadcasted_iota(I32, (CAP, CHIPS), 1).astype(F32)
    chosen = jnp.sum(jnp.where(slots == column(slot_row), picked, 0.0), axis=1, keepdims=True)
    total = jnp.sum(picked, axis=1, keepdims=True)
    live = total > 0.0
    return jnp.where(live, ROUTED_SCALE * (chosen / jnp.where(live, total, 1.0)), 0.0)


def spread(rows_h, spots_h, out_f, out_b, rows, spots, placed, load_sem, store_sem):
    loads = [
        pltpu.make_async_copy(spots_h, spots, load_sem.at[0]),
        pltpu.make_async_copy(rows_h.at[0], rows.at[0], load_sem.at[1]),
        pltpu.make_async_copy(rows_h.at[1], rows.at[1], load_sem.at[2]),
    ]
    for load in loads:
        load.start()
    loads[0].wait()
    stores = []
    for f, out in enumerate((out_f, out_b)):
        loads[1 + f].wait()
        total = None
        for e in range(EXPERTS):
            spot = placer(spots[f, pl.ds(e, 1), pl.ds(0, CAP)]).astype(BF16)
            term = dot(spot, rows[f, e], ((1,), (0,)))
            total = term if total is None else total + term
        placed[f] = total.astype(BF16)
        stores.append(pltpu.make_async_copy(placed.at[f], out.at[0], store_sem.at[f]))
        stores[f].start()
    for store in stores:
        store.wait()


def kernel(
    fin, sav, gra, wg_h, wu_h, wd_h, aff_h, lists_h, slots_h,
    out_p, out_l,
    aff, lists, slots, vx, wgu, wd, snd, rcv, lst, nlst,
    part_f, part_b, part_g, xs_gu, xr_gu, xs_g, xr_g,
    hid, sib_s, sib_r, own, mate_s, mate_r, com_s, com_r, pip_s, pip_r,
    load_sem, store_sem, dis_s, dis_r, fwd_s, fwd_r, dp_s, dp_r, ss_s, ss_r, ma_s, ma_r, co_s, co_r, pi_s, pi_r, li_s, li_r,
):
    p, x, d = lax.axis_index("pipe"), lax.axis_index("expert"), lax.axis_index("dp")
    pipes = lax.axis_size("pipe")
    z, c = lax.div(x, 2), lax.rem(x, 2)
    half = lax.div(z, HALF)
    sibling = (p, z * 2 + 1 - c, d)
    partner = (p, x, 1 - d)
    after = (lax.rem(p + 1, pipes), x, d)
    before = (lax.rem(p + pipes - 1, pipes), x, d)
    toward = 2 * lax.rem(z, 2) - 1
    chip = lambda k: lax.rem(z + CHIPS + k * toward, CHIPS)
    at_chip = lambda k: (p, chip(k) * 2 + c, d)
    goal = {1: 1, 2: -2, 3: 3}
    sent = []

    barrier = pltpu.get_barrier_semaphore()
    for peer in [at_chip(k) for k in PEERS] + [sibling, partner, after, before]:
        pl.semaphore_signal(barrier, inc=1, device_id=peer, device_id_type=MESH)

    loads = [
        pltpu.make_async_copy(src, dst, load_sem.at[i])
        for i, (src, dst) in enumerate([
            (fin.at[0], vx.at[0]), (sav.at[0], vx.at[1]), (gra.at[0], vx.at[2]),
            (wg_h.at[0], wgu.at[:, pl.ds(0, FF)]), (wu_h.at[0], wgu.at[:, pl.ds(FF, FF)]), (wd_h.at[0], wd),
            (lists_h, lists), (slots_h, slots), (aff_h, aff),
        ])
    ]
    for i in (6, 0, 1, 2, 7, 8, 3, 4, 5):
        loads[i].start()

    def remote(src, dst, send_sem, recv_sem, device):
        return pltpu.make_async_remote_copy(
            src_ref=src, dst_ref=dst, send_sem=send_sem, recv_sem=recv_sem, device_id=device, device_id_type=MESH
        )

    def send(*args):
        copy = remote(*args)
        copy.start()
        sent.append(copy)

    def pick(f):
        return [picker(lists[f, 0, 0, pl.ds(e, 1), :]) for e in range(EXPERTS)]

    def weigh(f, picks):
        return [entry_weight(picks[e], slots[f, 0, 0, pl.ds(e, 1), :], aff[f, 0]) for e in range(EXPERTS)]

    def gather(a, picks, weights=None):
        got = dot(jnp.concatenate(picks, axis=0).astype(BF16), vx[a], ((1,), (0,)))
        for e in range(EXPERTS):
            block = got[e * CAP : (e + 1) * CAP]
            if weights is not None:
                block = weights[e] * block
            snd[a, e] = block.astype(BF16)
        rcv[a, 0, 0] = snd[a, half]

    def dispatch(a):
        for k in STEPS:
            send(
                snd.at[a, lax.div(chip(goal[k]), HALF)], rcv.at[a, 0, k],
                dis_s.at[a, k], dis_r.at[a, k], at_chip(goal[k]),
            )
        send(snd.at[a, half], rcv.at[a, 0, 4], dis_s.at[a, 4], dis_r.at[a, 4], at_chip(-1))
        share(a, 0)

    def share(a, i):
        send(rcv.at[a, 0, i], rcv.at[a, 1, i], fwd_s.at[a, i], fwd_r.at[a, i], sibling)

    def arrived(a, i):
        remote(snd.at[a, 0], rcv.at[a, 0, i], dis_s.at[a, i], dis_r.at[a, i], sibling).wait_recv()

    def shared(a, first, last):
        for i in range(first, last):
            remote(snd.at[a, 0], rcv.at[a, 1, i], fwd_s.at[a, i], fwd_r.at[a, i], sibling).wait_recv()

    def relay(a):
        for k in (1, 2, 3):
            arrived(a, k)
            send(rcv.at[a, 0, k], rcv.at[a, 0, 4 + k], dis_s.at[a, 4 + k], dis_r.at[a, 4 + k], at_chip(-1))
            share(a, k)

    def collect_early(a):
        arrived(a, 4)
        share(a, 4)
        shared(a, 0, EARLY)

    def collect_late(a):
        for i in range(EARLY, CHIPS):
            arrived(a, i)
            share(a, i)
        shared(a, EARLY, CHIPS)

    def collect(a):
        arrived(a, 4)
        share(a, 4)
        collect_late(a)
        shared(a, 0, EARLY)

    def all_rows(a):
        return rcv[a].reshape(2 * CHIPS * CAP, rcv.shape[-1])

    loads[6].wait()
    picks = [pick(0)]
    loads[0].wait()
    gather(0, picks[0])
    pl.semaphore_wait(barrier, len(PEERS) + 4)
    dispatch(0)
    picks.append(pick(1))
    loads[1].wait()
    gather(1, picks[1])
    dispatch(1)
    loads[7].wait()
    loads[8].wait()
    loads[2].wait()
    gather(2, picks[1], weigh(1, picks[1]))
    lst[...] = jnp.zeros_like(lst)
    for f in range(2):
        lst[f, pl.ds(0, EXPERTS), pl.ds(0, CAP)] = lists[f, 0, 0]
    send(lst.at[0], nlst.at[0], li_s.at[0], li_r.at[0], after)
    send(lst.at[1], nlst.at[1], li_s.at[1], li_r.at[1], before)
    weights = weigh(0, picks[0])
    for load in loads[3:6]:
        load.wait()

    def exchange_gu(f, i=0, first=0, last=CHIPS):
        part = part_f if f == 0 else part_b
        rows = (last - first) * CAP
        at = pl.ds(first * CAP, rows)
        got = dot(rcv[f, :, pl.ds(first, last - first)].reshape(2 * rows, wd.shape[-1]), wgu[...], ((1,), (0,)))
        got = got.reshape(2, rows, 2 * FF)
        part[:, at, :] = got
        xs_gu[f, :, at, :] = got.astype(BF16)
        send(xs_gu.at[f, :, at], xr_gu.at[f, :, at], dp_s.at[f, i], dp_r.at[f, i], partner)

    def joined_gu(f, parts=((0, CHIPS),)):
        part = part_f if f == 0 else part_b
        for i, (first, last) in enumerate(parts):
            at = pl.ds(first * CAP, (last - first) * CAP)
            remote(xs_gu.at[f, :, at], xr_gu.at[f, :, at], dp_s.at[f, i], dp_r.at[f, i], partner).wait_recv()
        total = (part[...] + xr_gu[f].astype(F32)).reshape(2 * CHIPS * CAP, 2 * FF)
        return total[:, :FF], total[:, FF:]

    def product(f):
        for j, (at, width) in enumerate(CUTS[f]):
            cols = pl.ds(at, width)
            if f == 0:
                got = dot(hid[0, :, pl.ds(0, FF)], wd[:, cols], ((1,), (0,)))
            else:
                got = dot(hid[1], wgu[cols, :], ((1,), (1,)))
            got = got.reshape(2, CHIPS, CAP, width)
            sib_s[f, :, :, cols] = got[1].astype(BF16)
            for i, (first, last) in enumerate(SHARES):
                at = pl.ds(first, last - first)
                send(sib_s.at[f, at, :, cols], sib_r.at[f, at, :, cols], ss_s.at[f, j, i], ss_r.at[f, j, i], sibling)
            own[f, :, :, cols] = got[0]

    def gathered(f, i, cols):
        return own[f, i, :, cols] + sib_r[f, i, :, cols].astype(F32)

    def shared_sum(f, j, i):
        cols = pl.ds(*CUTS[f][j])
        first, last = SHARES[i]
        at = pl.ds(first, last - first)
        remote(
            sib_s.at[f, at, :, cols], sib_r.at[f, at, :, cols], ss_s.at[f, j, i], ss_r.at[f, j, i], sibling
        ).wait_recv()

    def to_mate(f, j):
        cols = pl.ds(*CUTS[f][j])
        for i, (first, last) in enumerate(SHARES[:1]):
            shared_sum(f, j, i)
        for k in STEPS:
            mate_s[f, k, :, cols] = gathered(f, 4 + k, cols).astype(BF16)
            send(mate_s.at[f, k, :, cols], mate_r.at[f, k, :, cols], ma_s.at[f, j, k], ma_r.at[f, j, k], at_chip(-1))

    def mate_own(f, j):
        cols = pl.ds(*CUTS[f][j])
        mate_s[f, 0, :, cols] = gathered(f, 4, cols).astype(BF16)
        send(mate_s.at[f, 0, :, cols], mate_r.at[f, 0, :, cols], ma_s.at[f, j, 0], ma_r.at[f, j, 0], at_chip(-1))

    def from_mate(f, j, k):
        cols = pl.ds(*CUTS[f][j])
        remote(mate_s.at[f, k, :, cols], mate_r.at[f, k, :, cols], ma_s.at[f, j, k], ma_r.at[f, j, k], sibling).wait_recv()
        return (gathered(f, k, cols) + mate_r[f, k, :, cols].astype(F32)).astype(BF16)

    def combine(f, j):
        cols = pl.ds(*CUTS[f][j])
        pair = lax.div(z, 2)
        shared_sum(f, j, 1)
        for k in STEPS:
            com_s[f, k, :, cols] = from_mate(f, j, k)
            send(com_s.at[f, k, :, cols], com_r.at[f, pair, :, cols], co_s.at[f, j, k], co_r.at[f, j, k], at_chip(k))
            if k == STEPS[0]:
                mate_own(f, j)
        com_r[f, pair, :, cols] = from_mate(f, j, 0)

    def hand_on(f, j):
        cols = pl.ds(*CUTS[f][j])
        for k in (1, 2, 3):
            source = lax.div(chip(goal[k]), 2)
            remote(
                com_s.at[f, k, :, cols], com_r.at[f, source, :, cols], co_s.at[f, j, k], co_r.at[f, j, k], sibling
            ).wait_recv()
        for e in range(EXPERTS):
            total = com_r[f, 2 * e, :, cols].astype(F32) + com_r[f, 2 * e + 1, :, cols].astype(F32)
            if f == 0:
                total = weights[e] * total
            pip_s[f, e, :, cols] = total.astype(BF16)
        send(
            pip_s.at[f, :, :, cols], pip_r.at[f, :, :, cols], pi_s.at[f, j], pi_r.at[f, j], after if f == 0 else before
        )

    stores = []

    def place(f, j):
        cols = pl.ds(*CUTS[f][j])
        if j == 0:
            remote(lst.at[f], nlst.at[f], li_s.at[f], li_r.at[f], after).wait_recv()
            copy = pltpu.make_async_copy(nlst.at[f], out_l.at[f], store_sem.at[f, 0])
            copy.start()
            stores.append(copy)
        remote(pip_s.at[f, :, :, cols], pip_r.at[f, :, :, cols], pi_s.at[f, j], pi_r.at[f, j], after).wait_recv()
        copy = pltpu.make_async_copy(pip_r.at[f, :, :, cols], out_p.at[f, :, :, cols], store_sem.at[f, 1 + j])
        copy.start()
        stores.append(copy)

    def exchange_grad(i, first, last):
        rows = (last - first) * CAP
        got = dot(rcv[2, :, pl.ds(first, last - first)].reshape(2 * rows, wd.shape[-1]), wd[...], ((1,), (1,)))
        got = got.reshape(2, rows, FF)
        at = pl.ds(first * CAP, rows)
        part_g[:, at, :] = got
        xs_g[:, at, :] = got.astype(BF16)
        send(xs_g.at[:, at], xr_g.at[:, at], dp_s.at[2, i], dp_r.at[2, i], partner)

    def joined_grad(i, first, last):
        at = pl.ds(first * CAP, (last - first) * CAP)
        remote(xs_g.at[:, at], xr_g.at[:, at], dp_s.at[2, i], dp_r.at[2, i], partner).wait_recv()

    relay(0)
    relay(1)
    dispatch(2)
    collect_early(0)
    exchange_gu(0, 0, *PARTS[0])
    collect_late(0)
    exchange_gu(0, 1, *PARTS[1])
    collect_early(1)
    exchange_gu(1, 0, *PARTS[0])
    relay(2)
    collect_late(1)
    exchange_gu(1, 1, *PARTS[1])
    gate, up = joined_gu(0, PARTS)
    hid[0, :, pl.ds(0, FF)] = (gate * jax.nn.sigmoid(gate) * up).astype(BF16)
    product(0)
    collect_early(2)
    exchange_grad(0, *PARTS[0])
    to_mate(0, 0)
    collect_late(2)
    exchange_grad(1, *PARTS[1])
    gate, up = joined_gu(1, PARTS)
    sg = jax.nn.sigmoid(gate)
    by_gate = up * sg * (1.0 + gate * (1.0 - sg))
    by_up = gate * sg
    combine(0, 0)
    joined_grad(0, *PARTS[0])
    joined_grad(1, *PARTS[1])
    grad = (part_g[...] + xr_g[...].astype(F32)).reshape(2 * CHIPS * CAP, FF)
    hid[1, :, pl.ds(0, FF)] = (grad * by_gate).astype(BF16)
    hid[1, :, pl.ds(FF, FF)] = (grad * by_up).astype(BF16)
    product(1)
    to_mate(1, 0)
    hand_on(0, 0)
    combine(1, 0)
    place(0, 0)
    hand_on(1, 0)
    place(1, 0)
    for copy in sent:
        copy.wait_send()
    for copy in stores:
        copy.wait()


def per_device(forward_input, saved_input, output_grad, gate_proj, up_proj, down_proj, affinity, token_lists, slot_ids):
    width = forward_input.shape[-1]
    whole = pl.BlockSpec(memory_space=pltpu.HBM)
    blocks = 2 * CHIPS
    entries = blocks * CAP
    dma = pltpu.SemaphoreType.DMA
    rows, spots = pl.pallas_call(
        kernel,
        out_shape=(
            jax.ShapeDtypeStruct((2, EXPERTS, CAP, width), BF16),
            jax.ShapeDtypeStruct((2, 8, TOK), I32),
        ),
        in_specs=[whole] * 9,
        out_specs=(whole, whole),
        scratch_shapes=[
            pltpu.VMEM((2, 1, CHIPS, TOK), F32),
            pltpu.VMEM((2, 1, 1, EXPERTS, CAP), I32),
            pltpu.VMEM((2, 1, 1, EXPERTS, CAP), I32),
            pltpu.VMEM((3, TOK, width), BF16),
            pltpu.VMEM((width, 2 * FF), BF16),
            pltpu.VMEM((FF, width), BF16),
            pltpu.VMEM((3, EXPERTS, CAP, width), BF16),
            pltpu.VMEM((3, 2, CHIPS, CAP, width), BF16),
            pltpu.VMEM((2, 8, 128), I32),
            pltpu.VMEM((2, 8, 128), I32),
            pltpu.VMEM((2, CHIPS * CAP, 2 * FF), F32),
            pltpu.VMEM((2, CHIPS * CAP, 2 * FF), F32),
            pltpu.VMEM((2, CHIPS * CAP, FF), F32),
            pltpu.VMEM((2, 2, CHIPS * CAP, 2 * FF), BF16),
            pltpu.VMEM((2, 2, CHIPS * CAP, 2 * FF), BF16),
            pltpu.VMEM((2, CHIPS * CAP, FF), BF16),
            pltpu.VMEM((2, CHIPS * CAP, FF), BF16),
            pltpu.VMEM((2, entries, 2 * FF), BF16),
            pltpu.VMEM((2, CHIPS, CAP, width), BF16),
            pltpu.VMEM((2, CHIPS, CAP, width), BF16),
            pltpu.VMEM((2, CHIPS, CAP, width), F32),
            pltpu.VMEM((2, 4, CAP, width), BF16),
            pltpu.VMEM((2, 4, CAP, width), BF16),
            pltpu.VMEM((2, 4, CAP, width), BF16),
            pltpu.VMEM((2, 4, CAP, width), BF16),
            pltpu.VMEM((2, EXPERTS, CAP, width), BF16),
            pltpu.VMEM((2, EXPERTS, CAP, width), BF16),
            dma((9,)), dma((2, 1 + MOST)),
            dma((3, CHIPS)), dma((3, CHIPS)), dma((3, CHIPS)), dma((3, CHIPS)),
            dma((3, 2)), dma((3, 2)), dma((2, MOST, 2)), dma((2, MOST, 2)), dma((2, MOST, 4)), dma((2, MOST, 4)),
            dma((2, MOST, 4)), dma((2, MOST, 4)), dma((2, MOST)), dma((2, MOST)), dma((2,)), dma((2,)),
        ],
        compiler_params=pltpu.CompilerParams(
            collective_id=0, has_side_effects=True, vmem_limit_bytes=VMEM_LIMIT
        ),
        cost_estimate=pl.CostEstimate(flops=2_000_000_000, bytes_accessed=6_000_000, transcendentals=262_144),
    )(
        forward_input, saved_input, output_grad, gate_proj, up_proj, down_proj,
        jnp.swapaxes(affinity, 2, 3), token_lists, slot_ids,
    )
    return pl.pallas_call(
        spread,
        out_shape=(jax.ShapeDtypeStruct((1, TOK, width), BF16),) * 2,
        in_specs=[whole] * 2,
        out_specs=(whole, whole),
        scratch_shapes=[
            pltpu.VMEM((2, EXPERTS, CAP, width), BF16),
            pltpu.VMEM((2, 8, TOK), I32),
            pltpu.VMEM((2, TOK, width), BF16),
            dma((3,)), dma((2,)),
        ],
        compiler_params=pltpu.CompilerParams(vmem_limit_bytes=VMEM_LIMIT),
    )(rows, spots)


def solution(mesh):
    in_specs = (
        P("pipe", "expert", "dp"),
        P("pipe", "expert", "dp"),
        P("pipe", "expert", "dp"),
        P("pipe", "dp", "expert"),
        P("pipe", "dp", "expert"),
        P("pipe", "expert", "dp"),
        P(None, "pipe", "expert", None),
        P(None, "pipe", "expert", None, None),
        P(None, "pipe", "expert", None, None),
    )
    out_specs = (P("pipe", "expert", "dp"), P("pipe", "expert", "dp"))
    return jax.shard_map(
        per_device, mesh=mesh, in_specs=in_specs, out_specs=out_specs, check_vma=False
    )
```

time: 74.7 us -> 69.4 us (0.929)
  the two profiles are of different devices: /device:TPU:26 before, /device:TPU:90 now
where the time goes in v3:
time: 69.4 us; the launch traced here: 69.2 us
  Pallas kernels  68.5 us (99%)
    pallas_call x1, Pallas kernels, per_device(): pl.pallas_call(kernel, out_shape=(jax.ShapeDtypeStruct((2, EXPERTS, CAP,...  66 us
    pallas_call x1, Pallas kernels, per_device(): pl.pallas_call(spread, out_shape=(jax.ShapeDtypeStruct((1, TOK, width), B...  2.53 us

profile of v3, /device:TPU:90, one launch (start us, length us, event | category | flops | bytes accessed | tf_op | source)
XLA Modules:
  0.0 69.2 jit_solution(12572986435758586271)
XLA Ops:
  0.6 66.0 %shard_map.104 = (bf16[2,2,16,1792]{3,2,1,0:T(8,128)(2,1)}, s32[2,8,128]{2,1,0:T(8,128)}) custom-call(bf16[1,128,1792]{2,1,0:T(8,128)(2,1)} %fin.1, bf16[1,128,1792]{2,1,0:T(8,128)(2,1)} %sav.1, bf16[1,128,1792]{2,1,0:T(8,128)(2,1)} %gra.1, bf16[1,1792,256]{2,1,0:T(8,128)(2,1)} %wg_h.1, bf16[1,1792,256]{2,1,0:T(8,128)(2,1)} %wu_h.1, ...), custom_call_target="tpu_custom_call" | custom-call | flops 2000000000 | bytes 6000000 | tf_op jit(solution)/shard_map/pallas_call | solution.py:376
  66.6 2.5 %shard_map.105 = (bf16[1,128,1792]{2,1,0:T(8,128)(2,1)}, bf16[1,128,1792]{2,1,0:T(8,128)(2,1)}) custom-call(bf16[2,2,16,1792]{3,2,1,0:T(8,128)(2,1)} %get-tuple-element.4.rows_h, s32[2,8,128]{2,1,0:T(8,128)} %get-tuple-element.5.spots_h), custom_call_target="tpu_custom_call" | custom-call | tf_op jit(solution)/shard_map/pallas_call | solution.py:425

commit v4 on v3

--- a/solution.py
+++ b/solution.py
@@ -18,7 +18,9 @@
 FF = 256
 VMEM_LIMIT = 62 * 1024 * 1024
 STEPS = (3, 2, 1)
-PEERS = (1, 2, 3, 4, -1, -2, -3)
+PEERS = (1, 2, 3, -1, -2)
+BEYOND = (0, 1, 2, 3, -2)
+MIRROR = {0: 0, 1: 1, 2: -2, 3: 3, -2: 2}
 EARLY = 5
 SHARES = ((5, 8), (0, 5))
 PARTS = ((0, EARLY), (EARLY, CHIPS))
@@ -82,10 +84,10 @@
 def kernel(
     fin, sav, gra, wg_h, wu_h, wd_h, aff_h, lists_h, slots_h,
     out_p, out_l,
-    aff, lists, slots, vx, wgu, wd, snd, rcv, lst, nlst,
+    aff, lists, slots, vx, wgu, wd, snd, rcv, lst, nlst, wei, nwei,
     part_f, part_b, part_g, xs_gu, xr_gu, xs_g, xr_g,
-    hid, sib_s, sib_r, own, mate_s, mate_r, com_s, com_r, pip_s, pip_r,
-    load_sem, store_sem, dis_s, dis_r, fwd_s, fwd_r, dp_s, dp_r, ss_s, ss_r, ma_s, ma_r, co_s, co_r, pi_s, pi_r, li_s, li_r,
+    hid, sib_s, sib_r, own, mate_s, mate_r, com_s, com_r, ended,
+    load_sem, store_sem, dis_s, dis_r, fwd_s, fwd_r, dp_s, dp_r, ss_s, ss_r, ma_s, ma_r, co_s, co_r, li_s, li_r, ready,
 ):
     p, x, d = lax.axis_index("pipe"), lax.axis_index("expert"), lax.axis_index("dp")
     pipes = lax.axis_size("pipe")
@@ -98,12 +100,36 @@
     toward = 2 * lax.rem(z, 2) - 1
     chip = lambda k: lax.rem(z + CHIPS + k * toward, CHIPS)
     at_chip = lambda k: (p, chip(k) * 2 + c, d)
-    goal = {1: 1, 2: -2, 3: 3}
+    goal = {0: 0, 1: 1, 2: -2, 3: 3}
+    far = lambda f, k: ((after, before)[f][0], chip(k) * 2 + c, d)
     sent = []
 
+    beyond = [(f, k) for f in range(2) for k in BEYOND]
+    higher = (after[0] > p, before[0] > p)
+
     barrier = pltpu.get_barrier_semaphore()
-    for peer in [at_chip(k) for k in PEERS] + [sibling, partner, after, before]:
+    for peer in [sibling, partner] + [at_chip(k) for k in PEERS]:
         pl.semaphore_signal(barrier, inc=1, device_id=peer, device_id_type=MESH)
+    for f, k in beyond:
+
+        @pl.when(higher[f])
+        def _(f=f, k=k):
+            pl.semaphore_signal(barrier, inc=1, device_id=far(f, k), device_id_type=MESH)
+
+    def enter():
+        lower = 2 - higher[0].astype(I32) - higher[1].astype(I32)
+        pl.semaphore_wait(barrier, len(PEERS) + 2 + len(BEYOND) * lower)
+        for f, k in beyond:
+
+            @pl.when(jnp.logical_not(higher[f]))
+            def _(f=f, k=k):
+                i = beyond.index((1 - f, MIRROR[k]))
+                pl.semaphore_signal(ready.at[i], inc=1, device_id=far(f, k), device_id_type=MESH)
+
+    def until_ready(f, k):
+        @pl.when(higher[f])
+        def _():
+            pl.semaphore_wait(ready.at[beyond.index((f, k))], 1)
 
     loads = [
         pltpu.make_async_copy(src, dst, load_sem.at[i])
@@ -113,7 +139,7 @@
             (lists_h, lists), (slots_h, slots), (aff_h, aff),
         ])
     ]
-    for i in (6, 0, 1, 2, 7, 8, 3, 4, 5):
+    for i in (6, 0, 1, 7, 8, 2):
         loads[i].start()
 
     def remote(src, dst, send_sem, recv_sem, device):
@@ -190,8 +216,10 @@
     picks = [pick(0)]
     loads[0].wait()
     gather(0, picks[0])
-    pl.semaphore_wait(barrier, len(PEERS) + 4)
+    enter()
     dispatch(0)
+    for i in (3, 4, 5):
+        loads[i].start()
     picks.append(pick(1))
     loads[1].wait()
     gather(1, picks[1])
@@ -203,9 +231,9 @@
     lst[...] = jnp.zeros_like(lst)
     for f in range(2):
         lst[f, pl.ds(0, EXPERTS), pl.ds(0, CAP)] = lists[f, 0, 0]
-    send(lst.at[0], nlst.at[0], li_s.at[0], li_r.at[0], after)
-    send(lst.at[1], nlst.at[1], li_s.at[1], li_r.at[1], before)
     weights = weigh(0, picks[0])
+    for e in range(EXPERTS):
+        wei[e] = jnp.broadcast_to(weights[e], (CAP, TOK))
     for load in loads[3:6]:
         load.wait()
 
@@ -272,18 +300,29 @@
 
     def combine(f, j):
         cols = pl.ds(*CUTS[f][j])
+        for k in (1, 2, 3):
+            until_ready(f, k)
         pair = lax.div(z, 2)
         shared_sum(f, j, 1)
         for k in STEPS:
             com_s[f, k, :, cols] = from_mate(f, j, k)
-            send(com_s.at[f, k, :, cols], com_r.at[f, pair, :, cols], co_s.at[f, j, k], co_r.at[f, j, k], at_chip(k))
+            send(com_s.at[f, k, :, cols], com_r.at[f, pair, :, cols], co_s.at[f, j, k], co_r.at[f, j, k], far(f, k))
             if k == STEPS[0]:
                 mate_own(f, j)
-        com_r[f, pair, :, cols] = from_mate(f, j, 0)
-
-    def hand_on(f, j):
-        cols = pl.ds(*CUTS[f][j])
-        for k in (1, 2, 3):
+        com_s[f, 0, :, cols] = from_mate(f, j, 0)
+        send(com_s.at[f, 0, :, cols], com_r.at[f, pair, :, cols], co_s.at[f, j, 0], co_r.at[f, j, 0], far(f, 0))
+
+    stores = []
+
+    def finish(f, j):
+        cols = pl.ds(*CUTS[f][j])
+        if j == 0:
+            remote(lst.at[f], nlst.at[f], li_s.at[f], li_r.at[f], after).wait_recv()
+            stores.append(pltpu.make_async_copy(nlst.at[f], out_l.at[f], store_sem.at[f, 0]))
+            stores[-1].start()
+            if f == 0:
+                remote(wei, nwei, li_s.at[2], li_r.at[2], after).wait_recv()
+        for k in (1, 2, 3, 0):
             source = lax.div(chip(goal[k]), 2)
             remote(
                 com_s.at[f, k, :, cols], com_r.at[f, source, :, cols], co_s.at[f, j, k], co_r.at[f, j, k], sibling
@@ -291,25 +330,10 @@
         for e in range(EXPERTS):
             total = com_r[f, 2 * e, :, cols].astype(F32) + com_r[f, 2 * e + 1, :, cols].astype(F32)
             if f == 0:
-                total = weights[e] * total
-            pip_s[f, e, :, cols] = total.astype(BF16)
-        send(
-            pip_s.at[f, :, :, cols], pip_r.at[f, :, :, cols], pi_s.at[f, j], pi_r.at[f, j], after if f == 0 else before
-        )
-
-    stores = []
-
-    def place(f, j):
-        cols = pl.ds(*CUTS[f][j])
-        if j == 0:
-            remote(lst.at[f], nlst.at[f], li_s.at[f], li_r.at[f], after).wait_recv()
-            copy = pltpu.make_async_copy(nlst.at[f], out_l.at[f], store_sem.at[f, 0])
-            copy.start()
-            stores.append(copy)
-        remote(pip_s.at[f, :, :, cols], pip_r.at[f, :, :, cols], pi_s.at[f, j], pi_r.at[f, j], after).wait_recv()
-        copy = pltpu.make_async_copy(pip_r.at[f, :, :, cols], out_p.at[f, :, :, cols], store_sem.at[f, 1 + j])
-        copy.start()
-        stores.append(copy)
+                total = nwei[e, :, pl.ds(0, 1)] * total
+            ended[f, e, :, cols] = total.astype(BF16)
+        stores.append(pltpu.make_async_copy(ended.at[f, :, :, cols], out_p.at[f, :, :, cols], store_sem.at[f, 1 + j]))
+        stores[-1].start()
 
     def exchange_grad(i, first, last):
         rows = (last - first) * CAP
@@ -336,6 +360,11 @@
     relay(2)
     collect_late(1)
     exchange_gu(1, 1, *PARTS[1])
+    for f in range(2):
+        until_ready(f, 0)
+    send(lst.at[0], nlst.at[0], li_s.at[0], li_r.at[0], after)
+    send(lst.at[1], nlst.at[1], li_s.at[1], li_r.at[1], before)
+    send(wei, nwei, li_s.at[2], li_r.at[2], after)
     gate, up = joined_gu(0, PARTS)
     hid[0, :, pl.ds(0, FF)] = (gate * jax.nn.sigmoid(gate) * up).astype(BF16)
     product(0)
@@ -344,11 +373,11 @@
     to_mate(0, 0)
     collect_late(2)
     exchange_grad(1, *PARTS[1])
+    combine(0, 0)
     gate, up = joined_gu(1, PARTS)
     sg = jax.nn.sigmoid(gate)
     by_gate = up * sg * (1.0 + gate * (1.0 - sg))
     by_up = gate * sg
-    combine(0, 0)
     joined_grad(0, *PARTS[0])
     joined_grad(1, *PARTS[1])
     grad = (part_g[...] + xr_g[...].astype(F32)).reshape(2 * CHIPS * CAP, FF)
@@ -356,11 +385,11 @@
     hid[1, :, pl.ds(FF, FF)] = (grad * by_up).astype(BF16)
     product(1)
     to_mate(1, 0)
-    hand_on(0, 0)
     combine(1, 0)
-    place(0, 0)
-    hand_on(1, 0)
-    place(1, 0)
+    finish(0, 0)
+    finish(1, 0)
+    for f in range(2):
+        until_ready(f, -2)
     for copy in sent:
         copy.wait_send()
     for copy in stores:
@@ -390,8 +419,10 @@
             pltpu.VMEM((FF, width), BF16),
             pltpu.VMEM((3, EXPERTS, CAP, width), BF16),
             pltpu.VMEM((3, 2, CHIPS, CAP, width), BF16),
-            pltpu.VMEM((2, 8, 128), I32),
-            pltpu.VMEM((2, 8, 128), I32),
+            pltpu.VMEM((2, 8, TOK), I32),
+            pltpu.VMEM((2, 8, TOK), I32),
+            pltpu.VMEM((EXPERTS, CAP, TOK), F32),
+            pltpu.VMEM((EXPERTS, CAP, TOK), F32),
             pltpu.VMEM((2, CHIPS * CAP, 2 * FF), F32),
             pltpu.VMEM((2, CHIPS * CAP, 2 * FF), F32),
             pltpu.VMEM((2, CHIPS * CAP, FF), F32),
@@ -408,11 +439,11 @@
             pltpu.VMEM((2, 4, CAP, width), BF16),
             pltpu.VMEM((2, 4, CAP, width), BF16),
             pltpu.VMEM((2, EXPERTS, CAP, width), BF16),
-            pltpu.VMEM((2, EXPERTS, CAP, width), BF16),
             dma((9,)), dma((2, 1 + MOST)),
             dma((3, CHIPS)), dma((3, CHIPS)), dma((3, CHIPS)), dma((3, CHIPS)),
             dma((3, 2)), dma((3, 2)), dma((2, MOST, 2)), dma((2, MOST, 2)), dma((2, MOST, 4)), dma((2, MOST, 4)),
-            dma((2, MOST, 4)), dma((2, MOST, 4)), dma((2, MOST)), dma((2, MOST)), dma((2,)), dma((2,)),
+            dma((2, MOST, 4)), dma((2, MOST, 4)), dma((3,)), dma((3,)),
+            pltpu.SemaphoreType.REGULAR((2 * len(BEYOND),)),
         ],
         compiler_params=pltpu.CompilerParams(
             collective_id=0, has_side_effects=True, vmem_limit_bytes=VMEM_LIMIT

time: 69.4 us -> 68.1 us (0.981)
  the two profiles are of different devices: /device:TPU:90 before, /device:TPU:50 now
where the time goes in v4:
time: 68.1 us; the launch traced here: 67.9 us
  Pallas kernels  67.2 us (99%)
    pallas_call x1, Pallas kernels, per_device(): pl.pallas_call(kernel, out_shape=(jax.ShapeDtypeStruct((2, EXPERTS, CAP,...  64.7 us
    pallas_call x1, Pallas kernels, per_device(): pl.pallas_call(spread, out_shape=(jax.ShapeDtypeStruct((1, TOK, width), B...  2.53 us

profile of v4, /device:TPU:50, one launch (start us, length us, event | category | flops | bytes accessed | tf_op | source)
XLA Modules:
  0.0 67.9 jit_solution(9969601056941352623)
XLA Ops:
  0.6 64.7 %shard_map.104 = (bf16[2,2,16,1792]{3,2,1,0:T(8,128)(2,1)}, s32[2,8,128]{2,1,0:T(8,128)}) custom-call(bf16[1,128,1792]{2,1,0:T(8,128)(2,1)} %fin.1, bf16[1,128,1792]{2,1,0:T(8,128)(2,1)} %sav.1, bf16[1,128,1792]{2,1,0:T(8,128)(2,1)} %gra.1, bf16[1,1792,256]{2,1,0:T(8,128)(2,1)} %wg_h.1, bf16[1,1792,256]{2,1,0:T(8,128)(2,1)} %wu_h.1, ...), custom_call_target="tpu_custom_call" | custom-call | flops 2000000000 | bytes 6000000 | tf_op jit(solution)/shard_map/pallas_call | solution.py:405
  65.3 2.5 %shard_map.105 = (bf16[1,128,1792]{2,1,0:T(8,128)(2,1)}, bf16[1,128,1792]{2,1,0:T(8,128)(2,1)}) custom-call(bf16[2,2,16,1792]{3,2,1,0:T(8,128)(2,1)} %get-tuple-element.4.rows_h, s32[2,8,128]{2,1,0:T(8,128)} %get-tuple-element.5.spots_h), custom_call_target="tpu_custom_call" | custom-call | tf_op jit(solution)/shard_map/pallas_call | solution.py:456

commit v5 on v4

--- a/solution.py
+++ b/solution.py
@@ -186,8 +186,8 @@
         for i in range(first, last):
             remote(snd.at[a, 0], rcv.at[a, 1, i], fwd_s.at[a, i], fwd_r.at[a, i], sibling).wait_recv()
 
-    def relay(a):
-        for k in (1, 2, 3):
+    def relay(a, steps=(1, 2, 3)):
+        for k in steps:
             arrived(a, k)
             send(rcv.at[a, 0, k], rcv.at[a, 0, 4 + k], dis_s.at[a, 4 + k], dis_r.at[a, 4 + k], at_chip(-1))
             share(a, k)
@@ -350,8 +350,8 @@
 
     relay(0)
     relay(1)
+    collect_early(0)
     dispatch(2)
-    collect_early(0)
     exchange_gu(0, 0, *PARTS[0])
     collect_late(0)
     exchange_gu(0, 1, *PARTS[1])

time: 68.1 us -> 67.8 us (level)
  the two profiles are of different devices: /device:TPU:50 before, /device:TPU:31 now
where the time goes in v5:
time: 67.8 us; the launch traced here: 67.6 us
  Pallas kernels  66.9 us (99%)
    pallas_call x1, Pallas kernels, per_device(): pl.pallas_call(kernel, out_shape=(jax.ShapeDtypeStruct((2, EXPERTS, CAP,...  64.4 us
    pallas_call x1, Pallas kernels, per_device(): pl.pallas_call(spread, out_shape=(jax.ShapeDtypeStruct((1, TOK, width), B...  2.53 us

profile of v5, /device:TPU:31, one launch (start us, length us, event | category | flops | bytes accessed | tf_op | source)
XLA Modules:
  0.0 67.6 jit_solution(4493396806375902447)
XLA Ops:
  0.6 64.4 %shard_map.104 = (bf16[2,2,16,1792]{3,2,1,0:T(8,128)(2,1)}, s32[2,8,128]{2,1,0:T(8,128)}) custom-call(bf16[1,128,1792]{2,1,0:T(8,128)(2,1)} %fin.1, bf16[1,128,1792]{2,1,0:T(8,128)(2,1)} %sav.1, bf16[1,128,1792]{2,1,0:T(8,128)(2,1)} %gra.1, bf16[1,1792,256]{2,1,0:T(8,128)(2,1)} %wg_h.1, bf16[1,1792,256]{2,1,0:T(8,128)(2,1)} %wu_h.1, ...), custom_call_target="tpu_custom_call" | custom-call | flops 2000000000 | bytes 6000000 | tf_op jit(solution)/shard_map/pallas_call | solution.py:405
  65.0 2.5 %shard_map.105 = (bf16[1,128,1792]{2,1,0:T(8,128)(2,1)}, bf16[1,128,1792]{2,1,0:T(8,128)(2,1)}) custom-call(bf16[2,2,16,1792]{3,2,1,0:T(8,128)(2,1)} %get-tuple-element.4.rows_h, s32[2,8,128]{2,1,0:T(8,128)} %get-tuple-element.5.spots_h), custom_call_target="tpu_custom_call" | custom-call | tf_op jit(solution)/shard_map/pallas_call | solution.py:456

commit v6 on v5

--- a/solution.py
+++ b/solution.py
@@ -224,16 +224,6 @@
     loads[1].wait()
     gather(1, picks[1])
     dispatch(1)
-    loads[7].wait()
-    loads[8].wait()
-    loads[2].wait()
-    gather(2, picks[1], weigh(1, picks[1]))
-    lst[...] = jnp.zeros_like(lst)
-    for f in range(2):
-        lst[f, pl.ds(0, EXPERTS), pl.ds(0, CAP)] = lists[f, 0, 0]
-    weights = weigh(0, picks[0])
-    for e in range(EXPERTS):
-        wei[e] = jnp.broadcast_to(weights[e], (CAP, TOK))
     for load in loads[3:6]:
         load.wait()
 
@@ -349,6 +339,10 @@
         remote(xs_g.at[:, at], xr_g.at[:, at], dp_s.at[2, i], dp_r.at[2, i], partner).wait_recv()
 
     relay(0)
+    loads[7].wait()
+    loads[8].wait()
+    loads[2].wait()
+    gather(2, picks[1], weigh(1, picks[1]))
     relay(1)
     collect_early(0)
     dispatch(2)
@@ -360,6 +354,12 @@
     relay(2)
     collect_late(1)
     exchange_gu(1, 1, *PARTS[1])
+    lst[...] = jnp.zeros_like(lst)
+    for f in range(2):
+        lst[f, pl.ds(0, EXPERTS), pl.ds(0, CAP)] = lists[f, 0, 0]
+    weights = weigh(0, picks[0])
+    for e in range(EXPERTS):
+        wei[e] = jnp.broadcast_to(weights[e], (CAP, TOK))
     for f in range(2):
         until_ready(f, 0)
     send(lst.at[0], nlst.at[0], li_s.at[0], li_r.at[0], after)

time: 67.8 us -> 68 us (level)
  no operation moved by 1% of the time
where the time goes in v6:
time: 68 us; the launch traced here: 67.8 us
  Pallas kernels  67.1 us (99%)
    pallas_call x1, Pallas kernels, per_device(): pl.pallas_call(kernel, out_shape=(jax.ShapeDtypeStruct((2, EXPERTS, CAP,...  64.6 us
    pallas_call x1, Pallas kernels, per_device(): pl.pallas_call(spread, out_shape=(jax.ShapeDtypeStruct((1, TOK, width), B...  2.54 us

profile of v6, /device:TPU:31, one launch (start us, length us, event | category | flops | bytes accessed | tf_op | source)
XLA Modules:
  0.0 67.8 jit_solution(732327906497496166)
XLA Ops:
  0.6 64.6 %shard_map.104 = (bf16[2,2,16,1792]{3,2,1,0:T(8,128)(2,1)}, s32[2,8,128]{2,1,0:T(8,128)}) custom-call(bf16[1,128,1792]{2,1,0:T(8,128)(2,1)} %fin.1, bf16[1,128,1792]{2,1,0:T(8,128)(2,1)} %sav.1, bf16[1,128,1792]{2,1,0:T(8,128)(2,1)} %gra.1, bf16[1,1792,256]{2,1,0:T(8,128)(2,1)} %wg_h.1, bf16[1,1792,256]{2,1,0:T(8,128)(2,1)} %wu_h.1, ...), custom_call_target="tpu_custom_call" | custom-call | flops 2000000000 | bytes 6000000 | tf_op jit(solution)/shard_map/pallas_call | solution.py:405
  65.2 2.5 %shard_map.105 = (bf16[1,128,1792]{2,1,0:T(8,128)(2,1)}, bf16[1,128,1792]{2,1,0:T(8,128)(2,1)}) custom-call(bf16[2,2,16,1792]{3,2,1,0:T(8,128)(2,1)} %get-tuple-element.4.rows_h, s32[2,8,128]{2,1,0:T(8,128)} %get-tuple-element.5.spots_h), custom_call_target="tpu_custom_call" | custom-call | tf_op jit(solution)/shard_map/pallas_call | solution.py:456
